TPU v7x, 128 devices: a whole 4x4x4 slice. The times are simulated.
128 devices in a mesh: inst: 16 (over z, x), tile: 8 (over y, core).
Axes of the slice: x: 4, y: 4, z: 4, core: 2. Of those that a mesh axis runs over, the one named last changes fastest.
Arguments:
- obs_values: bfloat16 [262144, 128], P(('inst', 'tile')), may hold values from -6 to 6
- obs_instrument: int32 [262144], P(('inst', 'tile')), may hold values from 0 to 15
- obs_target: int32 [262144, 1], P(('inst', 'tile')), may hold values from 0 to 127; in each aligned block of 2048 rows (0 to 2047, 2048 to 4095, ...) at most 32 rows name the same one
- obs_cell: int32 [262144], P(('inst', 'tile')), may hold values from 0 to 1023
- inst_bias: float32 [16, 128], replicated, may hold values from -5 to 5
- kernel: float32 [9, 128], replicated, may hold values from 0.1 to 1
- w_in: bfloat16 [128, 1024], replicated, may hold values from -0.5 to 0.5
- norm_gain: float32 [1024], replicated, may hold values from 0.1 to 1.9
- w_up: bfloat16 [1024, 1024], replicated, may hold values from -0.1875 to 0.1875
- w_down: bfloat16 [1024, 1024], replicated, may hold values from -0.1875 to 0.1875
- cotangent: bfloat16 [256, 512, 1024], P('tile', 'inst'), may hold values from -6 to 6
Outputs:
- predicted_field: bfloat16 [256, 512, 1024], P('tile', 'inst')
- grad_w_in: float32 [128, 1024], replicated
- grad_w_up: float32 [1024, 1024], replicated
- grad_w_down: float32 [1024, 1024], replicated
- grad_gain: float32 [1024], replicated
- filter_matrix_derivative: float32 [9, 128], replicated
- sensor_offset_derivative: float32 [16, 128], replicated
Inputs may be any that keep to these rules, and one draw needn't show every extreme that they name: `obs_target`: among the rows of one device no tile is named by more than 32 rows, a bound that some block reaches.
All inputs are finite; a program needn't handle non-finite values.
Results may differ from a plain program's by a relative error of at most 0.008.
Values may be sent and summed in bfloat16 or wider, within the bound.
A program may use at most 128 MiB of HBM per device.

v0:
```python
import jax
import jax.numpy as jnp
from jax import lax
from jax.experimental import pallas as pl
from jax.experimental.pallas import tpu as pltpu
from jax.sharding import PartitionSpec as P

offsets = [(a, b) for a in (-1, 0, 1) for b in (-1, 0, 1)]
f32, bf16 = jnp.float32, jnp.bfloat16


def inner(left, right, precision=None):
    return lax.dot_general(
        left,
        right,
        (((0,), (0,)), ((), ())),
        precision=precision,
        preferred_element_type=f32,
    )


def along(left, right):
    return lax.dot_general(left, right, (((1,), (1,)), ((), ())), preferred_element_type=f32)


MESH = pl.DeviceIdType.MESH
HALF = 1152
ROWS = 1024
STREAMS = (
    (0, 256, ("x", "y", "z")),
    (256, 128, ("y", "z", "x")),
    (384, 128, ("z", "x", "y")),
    (512, 128, ("x", "y", "z")),
    (640, 256, ("y", "z", "x")),
    (896, 128, ("z", "x", "y")),
    (1024, 128, ("z", "x", "y")),
)


def place():
    inst, tile = lax.axis_index("inst"), lax.axis_index("tile")
    return {"z": inst // 4, "x": inst % 4, "y": tile // 2, "core": tile % 2}


def device_at(at):
    return (at["z"] * 4 + at["x"], at["y"] * 2 + at["core"])


def moved(at, axis, step):
    size = 2 if axis == "core" else 4
    return {**at, axis: lax.rem(at[axis] + step, size)}


def send_to(source, landing, send_sem, recv_sem, to):
    copy = pltpu.make_async_remote_copy(
        src_ref=source,
        dst_ref=landing,
        send_sem=send_sem,
        recv_sem=recv_sem,
        device_id=to,
        device_id_type=MESH,
    )
    copy.start()
    return copy


def aligned(index, size):
    return pl.ds(pl.multiple_of(index * size, size), size)


class Stream:
    def __init__(self, number, at, t, o, bufs, send_sem, recv_sem):
        first, wide, self.order = STREAMS[number]
        self.cols = pl.ds(first, wide)
        self.wide = wide
        self.at, self.t, self.o = at, t, o
        self.core_in, self.core_sum, self.ins, self.outs = bufs
        self.sends, self.recvs = send_sem.at[number], recv_sem.at[number]
        self.started = []
        self.core = at["core"]

    def go(self, source, target, slot, at):
        copy = send_to(
            source, target, self.sends.at[slot], self.recvs.at[slot], device_at(at)
        )
        self.started.append(copy)
        return copy

    def core_scatter(self):
        other = moved(self.at, "core", 1)
        self.pending = [
            self.go(
                self.t.at[1 - self.core, :, self.cols], self.core_in.at[:, self.cols], 0, other
            )
        ]

    def core_add(self):
        for copy in self.pending:
            copy.wait_recv()
        step = 128

        def body(i, carry):
            rows = aligned(i, step)
            total = self.t[self.core, rows, self.cols].astype(f32) + self.core_in[
                rows, self.cols
            ].astype(f32)
            self.core_sum[rows, self.cols] = total.astype(bf16)
            return carry

        lax.fori_loop(0, ROWS // step, body, 0)

    def axis_scatter(self, level):
        axis, size = self.order[level], (256, 64, 16)[level]
        source = self.core_sum if level == 0 else self.outs[level - 1]
        self.pending = []
        for step in (1, 2, 3):
            peer = moved(self.at, axis, step)
            self.pending.append(
                self.go(
                    source.at[aligned(peer[axis], size), self.cols],
                    self.ins[level].at[step - 1, :, self.cols],
                    1 + 3 * level + step - 1,
                    peer,
                )
            )

    def axis_add(self, level):
        axis, size = self.order[level], (256, 64, 16)[level]
        source = self.core_sum if level == 0 else self.outs[level - 1]
        for copy in self.pending:
            copy.wait_recv()
        step = min(size, 64)

        def body(i, carry):
            rows = aligned(i, step)
            mine = pl.ds(pl.multiple_of(self.at[axis] * size + i * step, step), step)
            total = source[mine, self.cols].astype(f32)
            for j in range(3):
                total = total + self.ins[level][j, rows, self.cols].astype(f32)
            if level < 2:
                self.outs[level][rows, self.cols] = total.astype(bf16)
            else:
                self.o[self.core, self.owned(2), self.cols] = total.astype(bf16)
            return carry

        lax.fori_loop(0, size // step, body, 0)

    def owned(self, level):
        start = 0
        for axis, size in list(zip(self.order, (256, 64, 16)))[: level + 1]:
            start = start + self.at[axis] * size
        size = (256, 64, 16)[level]
        return pl.ds(pl.multiple_of(start, size), size)

    def axis_gather(self, level):
        axis = self.order[level]
        rows = self.owned(level)
        self.pending = []
        for step in (1, 2, 3):
            peer = moved(self.at, axis, step)
            part = self.o.at[self.core, rows, self.cols]
            self.pending.append(self.go(part, part, 10 + 3 * (2 - level) + step - 1, peer))

    def gather_wait(self):
        for copy in self.pending:
            copy.wait_recv()

    def core_gather(self):
        part = self.o.at[self.core, :, self.cols]
        self.pending = [self.go(part, part, 19, moved(self.at, "core", 1))]

    def finish(self):
        self.gather_wait()
        for copy in self.started:
            copy.wait_send()


def greet(at):
    barrier = pltpu.get_barrier_semaphore()
    peers = [moved(at, axis, step) for axis in ("x", "y", "z") for step in (1, 2, 3)]
    peers.append(moved(at, "core", 1))
    for peer in peers:
        pl.semaphore_signal(barrier, inc=1, device_id=device_at(peer), device_id_type=MESH)
    pl.semaphore_wait(barrier, len(peers))


def reduce_scratch():
    return [
        pltpu.VMEM((ROWS, HALF), bf16),
        pltpu.VMEM((ROWS, HALF), bf16),
        pltpu.VMEM((3, 256, HALF), bf16),
        pltpu.VMEM((3, 64, HALF), bf16),
        pltpu.VMEM((3, 16, HALF), bf16),
        pltpu.VMEM((256, HALF), bf16),
        pltpu.VMEM((64, HALF), bf16),
        pltpu.SemaphoreType.DMA((len(STREAMS), 20)),
        pltpu.SemaphoreType.DMA((len(STREAMS), 20)),
    ]


def reduce_kernel(t, o, core_in, core_sum, in0, in1, in2, out0, out1, send_sem, recv_sem):
    at = place()
    greet(at)
    bufs = (core_in, core_sum, (in0, in1, in2), (out0, out1))
    streams = [Stream(k, at, t, o, bufs, send_sem, recv_sem) for k in range(len(STREAMS))]
    for s in streams:
        s.core_scatter()
    for s in streams:
        s.core_add()
        s.axis_scatter(0)
    for level in (0, 1):
        for s in streams:
            s.axis_add(level)
            s.axis_scatter(level + 1)
    for s in streams:
        s.axis_add(2)
        s.axis_gather(2)
    for level in (1, 0):
        for s in streams:
            s.gather_wait()
            s.axis_gather(level)
    for s in streams:
        s.gather_wait()
        s.core_gather()
    for s in streams:
        s.finish()


def all_reduce(t):
    return pl.pallas_call(
        reduce_kernel,
        out_shape=jax.ShapeDtypeStruct((2, ROWS, HALF), bf16),
        in_specs=[pl.BlockSpec(memory_space=pltpu.VMEM)],
        out_specs=pl.BlockSpec(memory_space=pltpu.VMEM),
        scratch_shapes=reduce_scratch(),
        compiler_params=pltpu.CompilerParams(
            collective_id=0, has_side_effects=True, vmem_limit_bytes=56 << 20
        ),
    )(t)


def pack_grads(gw_down, gw_up, gw_in_t, g_gain, g_kernel, bias):
    small = jnp.concatenate([g_gain.reshape(8, 128), g_kernel, bias], axis=0)
    small = jnp.pad(small, ((0, ROWS - small.shape[0]), (0, 0)))
    halves = [
        jnp.concatenate([gw_down[:, :512], gw_up[:, :512], gw_in_t], axis=1),
        jnp.concatenate([gw_down[:, 512:], gw_up[:, 512:], small], axis=1),
    ]
    return jnp.stack(halves).astype(bf16)


def unpack_grads(o):
    gw_down = jnp.concatenate([o[0, :, :512], o[1, :, :512]], axis=1).astype(f32)
    gw_up = jnp.concatenate([o[0, :, 512:1024], o[1, :, 512:1024]], axis=1).astype(f32)
    gw_in = o[0, :, 1024:].T.astype(f32)
    small = o[1, :33, 1024:].astype(f32)
    return gw_in, gw_up, gw_down, small[:8].reshape(1024), small[8:17], small[17:33]


DEVICES, SLOTS, CH = 128, 32, 128
SIDE = 32
OBS_HERE = 2048


def iota(shape, axis):
    return lax.broadcasted_iota(jnp.int32, shape, axis)


def nt_dot(left, right):
    return lax.dot_general(left, right, (((1,), (1,)), ((), ())), preferred_element_type=f32)


def tn_dot(left, right):
    return lax.dot_general(left, right, (((0,), (0,)), ((), ())), preferred_element_type=f32)


def exchange_kernel(
    values,
    instr,
    target,
    cell,
    bias3,
    kern,
    enc,
    enc32,
    inv,
    pad_out,
    feat,
    places,
    packed,
    tags_out,
    got,
    tags_in,
    lands,
    right,
    spots,
    pad,
    cpad,
    side_out,
    side_in,
    corner_out,
    corner_in,
    sems,
    halo_send,
    halo_recv,
):
    inst, tile = lax.axis_index("inst"), lax.axis_index("tile")
    me = inst * 8 + tile
    barrier = pltpu.get_barrier_semaphore()

    def greet_one(i, carry):
        peer = lax.rem(me + i, DEVICES)
        pl.semaphore_signal(
            barrier, inc=1, device_id=(peer // 8, lax.rem(peer, 8)), device_id_type=MESH
        )
        return carry

    lax.fori_loop(1, DEVICES, greet_one, 0)

    block = 256
    upper = (iota((block, block), 0) < iota((block, block), 1)).astype(bf16)
    ahead = jnp.zeros((DEVICES, 1), f32)
    tags = jnp.zeros((DEVICES, CH), f32)
    for b in range(OBS_HERE // block):
        cols = slice(b * block, (b + 1) * block)
        to = target[:, cols]
        hit = (to == iota((DEVICES, block), 0)).astype(f32)
        hit16 = hit.astype(bf16)
        before = jnp.dot(hit16, upper, preferred_element_type=f32) + ahead
        slot = jnp.sum(hit * before, axis=0, keepdims=True)
        ahead = ahead + jnp.sum(hit, axis=1, keepdims=True)
        slot = slot.astype(jnp.int32)
        places[:, cols] = to * SLOTS + slot
        mine = (slot == iota((SLOTS, block), 0)).astype(f32)
        where = cell[:, cols]
        kind = instr[:, cols]
        notes = jnp.concatenate(
            [
                mine * (where // SIDE + 1).astype(f32),
                mine * (where % SIDE + 1).astype(f32),
                mine * (kind + 1).astype(f32),
                jnp.zeros((SLOTS, block), f32),
            ],
            axis=0,
        ).astype(bf16)
        tags = tags + nt_dot(hit16, notes)
        pick = (kind == iota((16, block), 0)).astype(f32)
        pick3 = jnp.concatenate([pick, pick, pick], axis=0).T.astype(bf16)
        offset = jnp.dot(pick3, bias3[...], preferred_element_type=f32)
        feat[cols, :] = (values[cols, :].astype(f32) + offset).astype(bf16)
    for t in range(DEVICES):
        tags_out[t] = tags[t : t + 1, :]

    pl.semaphore_wait(barrier, DEVICES - 1)

    group = 8 * SLOTS

    def pack_and_send(i, carry):
        tb = lax.rem(inst + i, 16)
        choose = (places[...] - tb * group == iota((group, OBS_HERE), 0)).astype(f32).astype(bf16)
        rows = jnp.dot(choose, feat[...], preferred_element_type=f32).astype(bf16)
        packed[pl.ds(pl.multiple_of(tb * 8, 8), 8)] = rows.reshape(8, SLOTS, CH)

        def send_one(j, inner_carry):
            to_tile = lax.rem(tile + j, 8)
            t = tb * 8 + to_tile

            @pl.when(t != me)
            def _():
                for source, landing, k in ((packed, got, 0), (tags_out, tags_in, 1)):
                    pltpu.make_async_remote_copy(
                        src_ref=source.at[t],
                        dst_ref=landing.at[me],
                        send_sem=sems.at[k],
                        recv_sem=sems.at[2 + k],
                        device_id=(tb, to_tile),
                        device_id_type=MESH,
                    ).start()

            return inner_carry

        lax.fori_loop(0, 8, send_one, 0)
        return carry

    lax.fori_loop(0, 16, pack_and_send, 0)
    got[me] = packed[me]
    tags_in[me] = tags_out[me]
    others = pl.ds(0, DEVICES - 1)
    pltpu.make_async_copy(tags_in.at[others], tags_in.at[others], sems.at[3]).wait()
    every = tags_in[...].reshape(DEVICES, CH)
    for k in range(3):
        spots[k] = jnp.concatenate(
            [every[SIDE * m : SIDE * (m + 1), 32 * k : 32 * (k + 1)] for m in range(4)], axis=1
        )

    def place_group(g, carry):
        row = pl.ds(g, 1)
        lat, lon, kind = (spots[k, row, :] for k in range(3))
        number = iota((SIDE, CH), 0).astype(f32) + 1.0
        at_lon = (lon == number).astype(f32)
        cols = aligned(g, CH)
        for p in range(SIDE):
            lands[p * SIDE : (p + 1) * SIDE, cols] = jnp.where(
                lat == float(p + 1), at_lon, 0.0
            ).astype(bf16)
        kinds = (kind == iota((CH, CH), 0).astype(f32) + 1.0).astype(f32).T.astype(bf16)
        right[aligned(g, CH), CH:] = kinds
        return carry

    lax.fori_loop(0, SIDE, place_group, 0)
    pltpu.make_async_copy(got.at[others], got.at[others], sems.at[2]).wait()

    def collect_rows(g, carry):
        for m in range(4):
            rows = pl.ds(pl.multiple_of(g * CH + m * SLOTS, SLOTS), SLOTS)
            right[rows, :CH] = got[g + SIDE * m]
        return carry

    lax.fori_loop(0, SIDE, collect_rows, 0)

    def sum_block(i, carry):
        total = jnp.dot(lands[aligned(i, 256), :], right[...], preferred_element_type=f32)
        pad[pl.ds(1 + 8 * i, 8), 8:40, :] = total.reshape(8, SIDE, 2 * CH)
        return carry

    lax.fori_loop(0, 4, sum_block, 0)

    for p in range(SIDE):
        side_out[0, p : p + 1, :] = pad[1 + p, 8:9, :]
        side_out[1, p : p + 1, :] = pad[1 + p, 39:40, :]
    for k, (p, q) in enumerate(((1, 8), (1, 39), (32, 8), (32, 39))):
        corner_out[k] = pad[p, q : q + 1, :]
    north, south = lax.rem(tile + 7, 8), lax.rem(tile + 1, 8)
    west, east = lax.rem(inst + 15, 16), lax.rem(inst + 1, 16)
    halo = (
        (pad.at[1, 8:40], pad.at[33, 8:40], (inst, north)),
        (pad.at[32, 8:40], pad.at[0, 8:40], (inst, south)),
        (side_out.at[0], side_in.at[1], (west, tile)),
        (side_out.at[1], side_in.at[0], (east, tile)),
        (corner_out.at[0], corner_in.at[3], (west, north)),
        (corner_out.at[1], corner_in.at[2], (east, north)),
        (corner_out.at[2], corner_in.at[1], (west, south)),
        (corner_out.at[3], corner_in.at[0], (east, south)),
    )
    copies = [
        send_to(source, landing, halo_send.at[k], halo_recv.at[k], to)
        for k, (source, landing, to) in enumerate(halo)
    ]
    for copy in copies:
        copy.wait_recv()
    keep_north = (tile > 0).astype(f32)
    keep_south = (tile < 7).astype(f32)
    keep_west = (inst > 0).astype(f32)
    keep_east = (inst < 15).astype(f32)
    pad[0, 8:40, :] = pad[0, 8:40, :] * keep_north
    pad[33, 8:40, :] = pad[33, 8:40, :] * keep_south
    for p in range(SIDE):
        pad[1 + p, 7:8, :] = side_in[0, p : p + 1, :] * keep_west
        pad[1 + p, 40:41, :] = side_in[1, p : p + 1, :] * keep_east
    pad[0, 7:8, :] = corner_in[0] * (keep_north * keep_west)
    pad[0, 40:41, :] = corner_in[1] * (keep_north * keep_east)
    pad[33, 7:8, :] = corner_in[2] * (keep_south * keep_west)
    pad[33, 40:41, :] = corner_in[3] * (keep_south * keep_east)

    def count(p, carry):
        total = jnp.sum(pad[p, :, CH:], axis=-1, keepdims=True)
        cpad[p] = jnp.broadcast_to(total, (48, CH))
        pad_out[p] = pad[p]
        return carry

    lax.fori_loop(0, 34, count, 0)

    def encode(p, carry):
        spread = jnp.zeros((SIDE, CH), f32)
        density = jnp.zeros((SIDE, CH), f32)
        for j, (a, b) in enumerate(offsets):
            weight = kern[j : j + 1, :]
            spread = spread + weight * pad[p + 1 + a, 8 + b : 40 + b, :CH]
            density = density + weight * cpad[p + 1 + a, 8 + b : 40 + b, :]
        share = 1.0 / (1.0 + density)
        value = spread * share
        inv[p] = share
        enc32[p] = value
        enc[aligned(p, SIDE), :] = value.astype(bf16)
        return carry

    lax.fori_loop(0, SIDE, encode, 0)
    for copy in copies:
        copy.wait_send()
    for source, k in ((packed, 0), (tags_out, 1)):
        pltpu.make_async_copy(source.at[others], source.at[others], sems.at[k]).wait()


def exchange(values, instr, target, cell, bias, kernel):
    hi = bias.astype(bf16)
    rest = bias - hi.astype(f32)
    mid = rest.astype(bf16)
    low = (rest - mid.astype(f32)).astype(bf16)
    bias3 = jnp.concatenate([hi, mid, low], axis=0)
    cells = SIDE * SIDE
    return pl.pallas_call(
        exchange_kernel,
        out_shape=(
            jax.ShapeDtypeStruct((cells, CH), bf16),
            jax.ShapeDtypeStruct((SIDE, SIDE, CH), f32),
            jax.ShapeDtypeStruct((SIDE, SIDE, CH), f32),
            jax.ShapeDtypeStruct((34, 48, 2 * CH), f32),
        ),
        in_specs=[pl.BlockSpec(memory_space=pltpu.VMEM)] * 6,
        out_specs=[pl.BlockSpec(memory_space=pltpu.VMEM)] * 4,
        scratch_shapes=[
            pltpu.VMEM((OBS_HERE, CH), bf16),
            pltpu.VMEM((1, OBS_HERE), jnp.int32),
            pltpu.VMEM((DEVICES, SLOTS, CH), bf16),
            pltpu.VMEM((DEVICES, 1, CH), f32),
            pltpu.VMEM((DEVICES, SLOTS, CH), bf16),
            pltpu.VMEM((DEVICES, 1, CH), f32),
            pltpu.VMEM((cells, DEVICES * SLOTS), bf16),
            pltpu.VMEM((DEVICES * SLOTS, 2 * CH), bf16),
            pltpu.VMEM((3, SIDE, CH), f32),
            pltpu.VMEM((34, 48, 2 * CH), f32),
            pltpu.VMEM((34, 48, CH), f32),
            pltpu.VMEM((2, SIDE, 2 * CH), f32),
            pltpu.VMEM((2, SIDE, 2 * CH), f32),
            pltpu.VMEM((4, 1, 2 * CH), f32),
            pltpu.VMEM((4, 1, 2 * CH), f32),
            pltpu.SemaphoreType.DMA((4,)),
            pltpu.SemaphoreType.DMA((8,)),
            pltpu.SemaphoreType.DMA((8,)),
        ],
        compiler_params=pltpu.CompilerParams(
            collective_id=1, has_side_effects=True, vmem_limit_bytes=56 << 20
        ),
    )(
        values,
        instr.reshape(1, OBS_HERE),
        target.reshape(1, OBS_HERE),
        cell.reshape(1, OBS_HERE),
        bias3,
        kernel,
    )


def shards(
    obs_values,
    obs_instrument,
    obs_target,
    obs_cell,
    inst_bias,
    kernel,
    w_in,
    norm_gain,
    w_up,
    w_down,
    cotangent,
):
    n_inst = lax.axis_size("inst")
    n_tile = lax.axis_size("tile")
    channels = obs_values.shape[1]
    lat_rows, lon_cols, width = cotangent.shape
    cells = lat_rows * lon_cols
    instruments = inst_bias.shape[0]
    enc, enc32, inv, padded = exchange(
        obs_values, obs_instrument, obs_target, obs_cell, inst_bias, kernel
    )
    psums, pkinds = padded[:, 7:41, :channels], padded[:, 7:41, channels : channels + instruments]
    pcounts = jnp.sum(pkinds, axis=2, keepdims=True)

    def shifted(padded, a, b):
        return padded[1 + a : 1 + a + lat_rows, 1 + b : 1 + b + lon_cols]

    h0 = jnp.dot(enc, w_in, preferred_element_type=f32)
    rinv = lax.rsqrt(jnp.mean(h0 * h0, axis=-1, keepdims=True) + 1e-06)
    normed = (h0 * rinv * norm_gain).astype(bf16)
    act = jnp.dot(normed, w_up, preferred_element_type=f32)
    gelu_out, gelu_back = jax.vjp(jax.nn.gelu, act)
    hidden = gelu_out.astype(bf16)
    predicted_field = (
        (h0 + jnp.dot(hidden, w_down, preferred_element_type=f32))
        .astype(bf16)
        .reshape(lat_rows, lon_cols, width)
    )
    scale = 1.0 / (lat_rows * n_tile * lon_cols * n_inst) ** 0.5
    dyb = (cotangent.astype(f32) * scale).astype(bf16).reshape(cells, width)
    gw_down = inner(hidden, dyb)
    dact = gelu_back(along(dyb, w_down))[0].astype(bf16)
    gw_up = inner(normed, dact)
    dnormed = along(dact, w_up)
    g_gain = jnp.sum(dnormed * h0 * rinv, axis=0)
    scaled = dnormed * norm_gain
    dh = (
        rinv * scaled
        - h0 * rinv**3 * jnp.mean(scaled * h0, axis=-1, keepdims=True)
        + dyb.astype(f32)
    ).astype(bf16)
    gw_in_t = inner(dh, enc)
    denc = along(dh, w_in).reshape(lat_rows, lon_cols, channels)
    dspread = denc * inv
    ddensity = -dspread * enc32
    kernel_rows = []
    bias = jnp.zeros((instruments, channels), f32)
    flat = dspread.reshape(cells, channels)
    for j, (a, b) in enumerate(offsets):
        near = shifted(pkinds, a, b)
        kernel_rows.append(
            jnp.sum(dspread * shifted(psums, a, b) + ddensity * shifted(pcounts, a, b), axis=(0, 1))
        )
        bias = bias + kernel[j] * inner(
            near.reshape(cells, instruments), flat, lax.Precision.HIGHEST
        )
    g_kernel = jnp.stack(kernel_rows)
    totals = unpack_grads(
        all_reduce(pack_grads(gw_down, gw_up, gw_in_t, g_gain, g_kernel, bias))
    )
    return (predicted_field, *totals)


def solution(mesh):
    return jax.shard_map(
        shards,
        mesh=mesh,
        in_specs=(
            P(("inst", "tile"), None),
            P(("inst", "tile")),
            P(("inst", "tile"), None),
            P(("inst", "tile")),
            P(),
            P(),
            P(),
            P(),
            P(),
            P(),
            P("tile", "inst", None),
        ),
        out_specs=(P("tile", "inst", None), P(), P(), P(), P(), P(), P()),
        check_vma=False,
    )
```

profile of v0, /device:TPU:1, one launch (start us, length us, event | category | flops | bytes accessed | tf_op | source)
XLA Modules:
  0.0 168.2 jit_solution(6124655085089248246)
XLA Ops:
  0.6 0.0 copy-start
  0.6 0.0 copy-start.8
  0.7 1.0 slice_bitcast_fusion.16
  1.6 0.8 fusion.41
  2.5 0.6 pad_maximum_fusion.1.bias3
  3.1 2.2 %multiply_convert_fusion = bf16[32,32,1024]{2,1,0:T(8,128)(2,1)S(1)} fusion(bf16[32,32,1024]{2,1,0:T(8,128)(2,1)} %param.21), kind=kLoop, calls=%fused_computation.15 | loop fusion | flops 3145728 | bytes 4194304 | tf_op jit(solution)/shard_map/convert_element_type | solution.py:584
  5.3 53.6 %shard_map.162 = (bf16[1024,128]{1,0:T(8,128)(2,1)}, f32[32,32,128]{2,1,0:T(8,128)}, f32[32,32,128]{2,1,0:T(8,128)}, f32[34,48,256]{2,1,0:T(8,128)}) custom-call(bf16[2048,128]{1,0:T(8,128)(2,1)} %values.1, s32[1,2048]{1,0:T(1,128)} %bitcast.178, s32[1,2048]{1,0:T(1,128)} %bitcast.179, s32[1,2048]{1,0:T(1,128)} %bitcast.180, ...), custom_call_target="tpu_custom_call" | custom-call | tf_op jit(solution)/shard_map/pallas_call | solution.py:501
  58.9 1.4 slice_reduce_fusion
  60.3 0.1 slice_bitcast_fusion.12
  60.4 0.0 copy-done.8
  60.4 0.0 copy-start.4
  60.4 0.0 copy-start.5
  60.4 2.4 %fusion.42 = f32[1024,1024]{1,0:T(8,128)S(1)} fusion(bf16[1024,1024]{1,0:T(8,128)(2,1)S(1)} %bitcast.175, bf16[1024,1024]{1,0:T(8,128)(2,1)S(1)} %copy-done.8), kind=kOutput, calls=%fused_computation.123 | convolution fusion | flops 2147483648 | bytes 8388608 | tf_op jit(solution)/shard_map/dot_general | solution.py:23
  62.8 0.0 copy-done.4
  62.8 0.0 copy-done.5
  62.8 0.0 copy-start.7
  62.8 0.8 multiply_reduce_fusion.2
  63.6 0.0 copy-done
  63.6 0.0 copy-done.7
  63.6 4.6 %fusion.7 = (bf16[1024,1024]{1,0:T(8,128)(2,1)S(1)}, f32[1024,1024]{1,0:T(8,128)S(1)}) fusion(f32[1024,1024]{1,0:T(8,128)S(1)} %fusion.42, bf16[1024,1024]{1,0:T(8,128)(2,1)S(1)} %copy-done, f32[1024,1024]{1,0:T(8,128)S(1)} %get-tuple-element.65, f32[1024]{0:T(1024)S(1)} %copy-done.7, f32[1024]{0:T(1024)S(1)} %get-tuple-element.63), kind=kOutput, calls=%fused_computation.11 | convolution fusion | flops 2171600896 | bytes 16785408 | tf_op jit(solution)/shard_map/dot_general | solution.py:575
  68.2 2.7 %convolution_convert_fusion = bf16[1024,1024]{1,0:T(8,128)(2,1)S(1)} fusion(bf16[1024,1024]{1,0:T(8,128)(2,1)S(1)} %get-tuple-element.66, f32[1024,1024]{1,0:T(8,128)S(1)} %get-tuple-element.65, f32[1024]{0:T(1024)S(1)} %copy-done.7, f32[1024]{0:T(1024)S(1)} %get-tuple-element.63), kind=kOutput, calls=%fused_computation.25 | convolution fusion | flops 2151677952 | bytes 8396800 | tf_op jit(solution)/shard_map/dot_general | solution.py:13
  70.9 0.0 copy-start.9
  70.9 1.1 fusion.40
  72.1 0.8 copy-done.9
  72.9 4.1 %add_convert_fusion.1 = bf16[1024,1024]{1,0:T(8,128)(2,1)} fusion(f32[1024,1024]{1,0:T(8,128)S(1)} %get-tuple-element.65, bf16[1024,1024]{1,0:T(8,128)(2,1)S(1)} %copy-done.9, f32[1024,1024]{1,0:T(8,128)S(1)} %get-tuple-element.67), kind=kOutput, calls=%fused_computation.16 | convolution fusion | flops 2159017984 | bytes 12582912 | tf_op jit(solution)/shard_map/dot_general | solution.py:579
  77.0 3.0 %convolution_convert_fusion.1 = bf16[1024,1024]{1,0:T(8,128)(2,1)S(1)} fusion(bf16[1024,1024]{1,0:T(8,128)(2,1)S(1)} %bitcast.176, f32[1024,1024]{1,0:T(8,128)S(1)} %get-tuple-element.67), kind=kOutput, calls=%fused_computation.26 | convolution fusion | flops 2157969408 | bytes 8388608 | tf_op jit(solution)/shard_map/dot_general | solution.py:13
  80.0 1.5 fusion.39
  81.5 2.7 %multiply_reduce_fusion.1 = (f32[1024]{0:T(1024)S(1)}, bf16[1024]{0:T(1024)(128)(2,1)S(1)}, f32[1024,1024]{1,0:T(8,128)S(1)}) fusion(f32[1024,1024]{1,0:T(8,128)S(1)} %get-tuple-element.65, f32[1024]{0:T(1024)S(1)} %copy-done.7, f32[1024]{0:T(1024)S(1)} %get-tuple-element.63, bf16[1024,1024]{1,0:T(8,128)(2,1)S(1)} %get-tuple-element.66, ...), kind=kOutput, calls=%fused_computation.14 | convolution fusion | flops 2153773056 | bytes 12597248 | tf_op jit(solution)/shard_map/dot_general | solution.py:23
  84.2 1.6 add_convert_fusion
  85.8 0.0 copy-start.1
  85.8 0.0 copy-start.3
  85.8 0.0 copy-start.6
  85.8 0.8 convolution_convert_fusion.2
  86.6 0.7 fusion.43
  87.3 0.0 copy-done.1
  87.3 0.0 copy-done.3
  87.4 0.2 copy-done.6
  87.5 1.9 %add_reduce_fusion = (bf16[128]{0:T(256)(128)(2,1)S(1)}, bf16[128]{0:T(256)(128)(2,1)S(1)}, bf16[128]{0:T(256)(128)(2,1)S(1)}, bf16[128]{0:T(256)(128)(2,1)S(1)}...) fusion(f32[34,48,256]{2,1,0:T(8,128)S(1)} %copy-done.1, ...), kind=kLoop, calls=%fused_computation.70 | loop fusion | flops 4586496 | bytes 6326272 | tf_op jit(solution)/shard_map/reduce_sum | solution.py:606
  89.5 0.3 add_reduce_fusion.8
  89.8 1.0 fusion.26
  90.8 1.0 fusion.25
  91.8 1.0 fusion.23
  92.8 1.0 fusion.21
  93.8 1.0 fusion.19
  94.8 1.0 fusion.17
  95.9 1.0 fusion.15
  96.9 1.0 fusion.13
  97.9 1.0 fusion.27
  98.9 0.2 concatenate.23
  99.1 2.1 %fusion.9 = (bf16[1,1024,1152]{2,1,0:T(8,128)(2,1)S(1)}, bf16[1,1024,1152]{2,1,0:T(8,128)(2,1)S(1)}) fusion(bf16[33,128]{1,0:T(8,128)(2,1)S(1)} %concatenate.23, bf16[1024,512]{1,0:T(8,128)(2,1)} %get-tuple-element.40, bf16[1024,512]{1,0:T(8,128)(2,1)} %get-tuple-element.38, bf16[1024,128]{1,0:T(8,128)(2,1)S(1)} %convolution_convert_fusion.2, ...), kind=kLoop, calls=%fused_computation.21 | loop fusion | flops 16515072 | bytes 9183488 | tf_op jit(solution)/shard_map/stack | solution.py:249
  101.1 2.6 %pad_maximum_fusion.t = bf16[2,1024,1152]{2,1,0:T(8,128)(2,1)} fusion(bf16[1,1024,1152]{2,1,0:T(8,128)(2,1)S(1)} %get-tuple-element.69, bf16[1,1024,1152]{2,1,0:T(8,128)(2,1)S(1)} %get-tuple-element.70), kind=kLoop, calls=%fused_computation.3 | loop fusion | flops 2359296 | bytes 9437184 | tf_op jit(solution)/shard_map/stack | solution.py:249
  103.8 47.4 %shard_map.163 = bf16[2,1024,1152]{2,1,0:T(8,128)(2,1)} custom-call(bf16[2,1024,1152]{2,1,0:T(8,128)(2,1)} %pad_maximum_fusion.t), custom_call_target="tpu_custom_call" | custom-call | tf_op jit(solution)/shard_map/pallas_call | solution.py:230
  151.2 0.7 slice_convert_fusion
  151.9 0.6 slice_bitcast_fusion.15
  152.5 0.6 slice_bitcast_fusion.13
  153.1 0.6 slice_bitcast_fusion.14
  153.7 1.8 %convert_bitcast_fusion = f32[128,1024]{0,1:T(8,128)} fusion(bf16[2,1024,1152]{2,1,0:T(8,128)(2,1)} %shard_map.163), kind=kLoop, calls=%fused_computation.60 | loop fusion | flops 131072 | bytes 786432 | tf_op jit(solution)/shard_map/convert_element_type | solution.py:255
  155.4 3.9 %slice_bitcast_fusion.1 = (bf16[1024,512]{1,0:T(8,128)(2,1)}, bf16[1024,512]{1,0:T(8,128)(2,1)}, bf16[1024,512]{1,0:T(8,128)(2,1)S(1)}, bf16[1024,512]{1,0:T(8,128)(2,1)}) fusion(bf16[2,1024,1152]{2,1,0:T(8,128)(2,1)} %shard_map.163), kind=kLoop, calls=%fused_computation.56 | loop fusion | bytes 8388608 | tf_op jit(solution)/shard_map/squeeze | solution.py:253
  159.4 2.0 %copy.30 = f32[128,1024]{1,0:T(8,128)} copy(f32[128,1024]{0,1:T(8,128)} %convert_bitcast_fusion) | data formatting | bytes 1048576
  161.4 0.0 copy-start.2
  161.4 4.2 %maximum_convert_fusion.1 = f32[1024,1024]{1,0:T(8,128)} fusion(bf16[1024,512]{1,0:T(8,128)(2,1)} %get-tuple-element.34, bf16[1024,512]{1,0:T(8,128)(2,1)} %get-tuple-element.33), kind=kLoop, calls=%fused_computation.24 | loop fusion | flops 4194304 | bytes 6291456 | tf_op jit(solution)/shard_map/convert_element_type | solution.py:253
  165.6 0.0 copy-done.2
  165.6 2.6 %maximum_convert_fusion = f32[1024,1024]{1,0:T(8,128)} fusion(bf16[1024,512]{1,0:T(8,128)(2,1)S(1)} %get-tuple-element.35, bf16[1024,512]{1,0:T(8,128)(2,1)S(1)} %copy-done.2), kind=kLoop, calls=%fused_computation.23 | loop fusion | flops 4194304 | bytes 6291456 | tf_op jit(solution)/shard_map/convert_element_type | solution.py:254
  (2 shorter events, 0.0 us)
Async XLA Ops:
  0.6 63.0 %copy-start = (bf16[1024,1024]{1,0:T(8,128)(2,1)S(1)}, bf16[1024,1024]{1,0:T(8,128)(2,1)}, u32[]{:S(2)}) copy-start(bf16[1024,1024]{1,0:T(8,128)(2,1)} %param.19) | copy-start | bytes 6291460
  0.6 59.8 %copy-start.8 = (bf16[1024,1024]{1,0:T(8,128)(2,1)S(1)}, bf16[1024,1024]{1,0:T(8,128)(2,1)}, u32[]{:S(2)}) copy-start(bf16[1024,1024]{1,0:T(8,128)(2,1)} %param.20) | copy-start | bytes 6291460
  60.4 2.4 %copy-start.4 = (bf16[1024,128]{1,0:T(8,128)(2,1)S(1)}, bf16[1024,128]{1,0:T(8,128)(2,1)}, u32[]{:S(2)}) copy-start(bf16[1024,128]{1,0:T(8,128)(2,1)} %get-tuple-element.11) | copy-start | bytes 786436
  60.4 2.4 %copy-start.5 = (bf16[128,1024]{1,0:T(8,128)(2,1)S(1)}, bf16[128,1024]{1,0:T(8,128)(2,1)}, u32[]{:S(2)}) copy-start(bf16[128,1024]{1,0:T(8,128)(2,1)} %param.17) | copy-start | bytes 786436
  62.8 0.8 copy-start.7
  70.9 2.0 %copy-start.9 = (bf16[1024,1024]{1,0:T(8,128)(2,1)S(1)}, bf16[1024,1024]{1,0:T(8,128)(2,1)}, u32[]{:S(2)}) copy-start(bf16[1024,1024]{1,0:T(8,128)(2,1)} %param.20) | copy-start | bytes 6291460
  85.8 1.5 copy-start.1
  85.8 1.5 copy-start.3
  85.8 1.7 copy-start.6
  161.4 4.2 %copy-start.2 = (bf16[1024,512]{1,0:T(8,128)(2,1)S(1)}, bf16[1024,512]{1,0:T(8,128)(2,1)}, u32[]{:S(2)}) copy-start(bf16[1024,512]{1,0:T(8,128)(2,1)} %get-tuple-element.36) | copy-start | bytes 3145732
where the time goes:
time: 169 us; the launch traced here: 168 us
  Pallas kernels  101 us (60%)
  matrix products  30.8 us (18%)
  other arithmetic  22.9 us (14%)
  local copies, waits for them, and re-layouts  12.7 us (8%)
    pallas_call x1, Pallas kernels, exchange(): pl.pallas_call(exchange_kernel, out_shape=(jax.ShapeDtypeStruct((cells, C...  53.6 us
    pallas_call x1, Pallas kernels, all_reduce(): pl.pallas_call(reduce_kernel, out_shape=jax.ShapeDtypeStruct((2, ROWS, HA...  47.4 us
    dot_general x12, matrix products, inner(): lax.dot_general(left, right, (((0,), (0,)), ((), ())), precision=precisio...  15.5 us
    dot_general x3, matrix products, along(): lax.dot_general(left, right, (((1,), (1,)), ((), ())), preferred_element_...  5.8 us
    another operation x2, other arithmetic, pack_grads(): return jnp.stack(halves).astype(bf16)  4.7 us
    dot_general x1, matrix products, shards(): act = jnp.dot(normed, w_up, preferred_element_type=f32)  4.6 us
    convert_element_type x1, other arithmetic, unpack_grads(): jnp.concatenate([o[0, :, :512], o[1, :, :512]], axis=1).astype(f32)  4.2 us
    dot_general x1, matrix products, shards(): jnp.dot(hidden, w_down, preferred_element_type=f32)  4.09 us

commit v1 on v0

--- a/solution.py
+++ b/solution.py
@@ -1,3 +1,5 @@
+import functools
+
 import jax
 import jax.numpy as jnp
 from jax import lax
@@ -9,31 +11,17 @@
 f32, bf16 = jnp.float32, jnp.bfloat16
 
 
-def inner(left, right, precision=None):
-    return lax.dot_general(
-        left,
-        right,
-        (((0,), (0,)), ((), ())),
-        precision=precision,
-        preferred_element_type=f32,
-    )
-
-
-def along(left, right):
-    return lax.dot_general(left, right, (((1,), (1,)), ((), ())), preferred_element_type=f32)
-
-
 MESH = pl.DeviceIdType.MESH
 HALF = 1152
 ROWS = 1024
 STREAMS = (
-    (0, 256, ("x", "y", "z")),
-    (256, 128, ("y", "z", "x")),
-    (384, 128, ("z", "x", "y")),
-    (512, 128, ("x", "y", "z")),
-    (640, 256, ("y", "z", "x")),
-    (896, 128, ("z", "x", "y")),
-    (1024, 128, ("z", "x", "y")),
+    (0, 256, ("x", "y", "z"), 0, 0),
+    (256, 128, ("y", "z", "x"), 0, 256),
+    (384, 128, ("z", "x", "y"), 0, 384),
+    (512, 128, ("x", "y", "z"), 1, 0),
+    (640, 256, ("y", "z", "x"), 1, 128),
+    (896, 128, ("z", "x", "y"), 1, 384),
+    (1024, 128, ("z", "x", "y"), 2, 0),
 )
 
 
@@ -69,11 +57,12 @@
 
 
 class Stream:
-    def __init__(self, number, at, t, o, bufs, send_sem, recv_sem):
-        first, wide, self.order = STREAMS[number]
+    def __init__(self, number, at, t, outs, bufs, send_sem, recv_sem):
+        first, wide, self.order, output, first_out = STREAMS[number]
         self.cols = pl.ds(first, wide)
-        self.wide = wide
-        self.at, self.t, self.o = at, t, o
+        self.at, self.t, self.o = at, t, outs[output]
+        half = self.o.shape[1] // 2
+        self.out_cols = pl.ds(pl.multiple_of(at["core"] * half + first_out, 128), wide)
         self.core_in, self.core_sum, self.ins, self.outs = bufs
         self.sends, self.recvs = send_sem.at[number], recv_sem.at[number]
         self.started = []
@@ -140,7 +129,7 @@
             if level < 2:
                 self.outs[level][rows, self.cols] = total.astype(bf16)
             else:
-                self.o[self.core, self.owned(2), self.cols] = total.astype(bf16)
+                self.o[self.owned(2), self.out_cols] = total.astype(bf16)
             return carry
 
         lax.fori_loop(0, size // step, body, 0)
@@ -158,7 +147,7 @@
         self.pending = []
         for step in (1, 2, 3):
             peer = moved(self.at, axis, step)
-            part = self.o.at[self.core, rows, self.cols]
+            part = self.o.at[rows, self.out_cols]
             self.pending.append(self.go(part, part, 10 + 3 * (2 - level) + step - 1, peer))
 
     def gather_wait(self):
@@ -166,7 +155,7 @@
             copy.wait_recv()
 
     def core_gather(self):
-        part = self.o.at[self.core, :, self.cols]
+        part = self.o.at[:, self.out_cols]
         self.pending = [self.go(part, part, 19, moved(self.at, "core", 1))]
 
     def finish(self):
@@ -196,65 +185,6 @@
         pltpu.SemaphoreType.DMA((len(STREAMS), 20)),
         pltpu.SemaphoreType.DMA((len(STREAMS), 20)),
     ]
-
-
-def reduce_kernel(t, o, core_in, core_sum, in0, in1, in2, out0, out1, send_sem, recv_sem):
-    at = place()
-    greet(at)
-    bufs = (core_in, core_sum, (in0, in1, in2), (out0, out1))
-    streams = [Stream(k, at, t, o, bufs, send_sem, recv_sem) for k in range(len(STREAMS))]
-    for s in streams:
-        s.core_scatter()
-    for s in streams:
-        s.core_add()
-        s.axis_scatter(0)
-    for level in (0, 1):
-        for s in streams:
-            s.axis_add(level)
-            s.axis_scatter(level + 1)
-    for s in streams:
-        s.axis_add(2)
-        s.axis_gather(2)
-    for level in (1, 0):
-        for s in streams:
-            s.gather_wait()
-            s.axis_gather(level)
-    for s in streams:
-        s.gather_wait()
-        s.core_gather()
-    for s in streams:
-        s.finish()
-
-
-def all_reduce(t):
-    return pl.pallas_call(
-        reduce_kernel,
-        out_shape=jax.ShapeDtypeStruct((2, ROWS, HALF), bf16),
-        in_specs=[pl.BlockSpec(memory_space=pltpu.VMEM)],
-        out_specs=pl.BlockSpec(memory_space=pltpu.VMEM),
-        scratch_shapes=reduce_scratch(),
-        compiler_params=pltpu.CompilerParams(
-            collective_id=0, has_side_effects=True, vmem_limit_bytes=56 << 20
-        ),
-    )(t)
-
-
-def pack_grads(gw_down, gw_up, gw_in_t, g_gain, g_kernel, bias):
-    small = jnp.concatenate([g_gain.reshape(8, 128), g_kernel, bias], axis=0)
-    small = jnp.pad(small, ((0, ROWS - small.shape[0]), (0, 0)))
-    halves = [
-        jnp.concatenate([gw_down[:, :512], gw_up[:, :512], gw_in_t], axis=1),
-        jnp.concatenate([gw_down[:, 512:], gw_up[:, 512:], small], axis=1),
-    ]
-    return jnp.stack(halves).astype(bf16)
-
-
-def unpack_grads(o):
-    gw_down = jnp.concatenate([o[0, :, :512], o[1, :, :512]], axis=1).astype(f32)
-    gw_up = jnp.concatenate([o[0, :, 512:1024], o[1, :, 512:1024]], axis=1).astype(f32)
-    gw_in = o[0, :, 1024:].T.astype(f32)
-    small = o[1, :33, 1024:].astype(f32)
-    return gw_in, gw_up, gw_down, small[:8].reshape(1024), small[8:17], small[17:33]
 
 
 DEVICES, SLOTS, CH = 128, 32, 128
@@ -295,7 +225,6 @@
     right,
     spots,
     pad,
-    cpad,
     side_out,
     side_in,
     corner_out,
@@ -315,6 +244,11 @@
         )
         return carry
 
+    def clear(p, carry):
+        pad[p] = jnp.zeros((48, 2 * CH), f32)
+        return carry
+
+    lax.fori_loop(0, 34, clear, 0)
     lax.fori_loop(1, DEVICES, greet_one, 0)
 
     block = 256
@@ -464,8 +398,8 @@
 
     def count(p, carry):
         total = jnp.sum(pad[p, :, CH:], axis=-1, keepdims=True)
-        cpad[p] = jnp.broadcast_to(total, (48, CH))
-        pad_out[p] = pad[p]
+        pad_out[p, :, : 2 * CH] = pad[p]
+        pad_out[p, :, 2 * CH :] = jnp.broadcast_to(total, (48, CH))
         return carry
 
     lax.fori_loop(0, 34, count, 0)
@@ -476,7 +410,7 @@
         for j, (a, b) in enumerate(offsets):
             weight = kern[j : j + 1, :]
             spread = spread + weight * pad[p + 1 + a, 8 + b : 40 + b, :CH]
-            density = density + weight * cpad[p + 1 + a, 8 + b : 40 + b, :]
+            density = density + weight * pad_out[p + 1 + a, 8 + b : 40 + b, 2 * CH :]
         share = 1.0 / (1.0 + density)
         value = spread * share
         inv[p] = share
@@ -504,7 +438,7 @@
             jax.ShapeDtypeStruct((cells, CH), bf16),
             jax.ShapeDtypeStruct((SIDE, SIDE, CH), f32),
             jax.ShapeDtypeStruct((SIDE, SIDE, CH), f32),
-            jax.ShapeDtypeStruct((34, 48, 2 * CH), f32),
+            jax.ShapeDtypeStruct((34, 48, 3 * CH), f32),
         ),
         in_specs=[pl.BlockSpec(memory_space=pltpu.VMEM)] * 6,
         out_specs=[pl.BlockSpec(memory_space=pltpu.VMEM)] * 4,
@@ -519,7 +453,6 @@
             pltpu.VMEM((DEVICES * SLOTS, 2 * CH), bf16),
             pltpu.VMEM((3, SIDE, CH), f32),
             pltpu.VMEM((34, 48, 2 * CH), f32),
-            pltpu.VMEM((34, 48, CH), f32),
             pltpu.VMEM((2, SIDE, 2 * CH), f32),
             pltpu.VMEM((2, SIDE, 2 * CH), f32),
             pltpu.VMEM((4, 1, 2 * CH), f32),
@@ -541,6 +474,360 @@
     )
 
 
+WIDTH = 1024
+CELLS = SIDE * SIDE
+TANH_SCALE = 0.7978845608028654
+CUBIC = 0.044715
+
+
+def small_reduce(at, axis, level, mine, boxes, send_sem, recv_sem):
+    size = 2 if axis == "core" else 4
+    boxes[level, at[axis]] = mine
+    copies = []
+    for step in range(1, size):
+        box = boxes.at[level, at[axis]]
+        k = 3 * level + step - 1
+        copies.append(
+            send_to(box, box, send_sem.at[k], recv_sem.at[k], device_at(moved(at, axis, step)))
+        )
+    return copies
+
+
+def small_total(axis, level, boxes, copies):
+    for copy in copies:
+        copy.wait_recv()
+    total = boxes[level, 0]
+    for k in range(1, 2 if axis == "core" else 4):
+        total = total + boxes[level, k]
+    return total
+
+
+def train_kernel(
+    scale,
+    enc,
+    enc32,
+    inv,
+    pad,
+    kern,
+    gain,
+    w_in_hbm,
+    w_up_hbm,
+    w_down_hbm,
+    cot_hbm,
+    y_hbm,
+    o_down,
+    o_up,
+    o_in,
+    o_small,
+    w_in,
+    w_up,
+    w_down,
+    dyb,
+    h0,
+    rinv,
+    u,
+    g,
+    dact,
+    ds,
+    dz,
+    gain_sum,
+    boxes,
+    t,
+    load_sem,
+    small_send,
+    small_recv,
+    core_in,
+    core_sum,
+    in0,
+    in1,
+    in2,
+    out0,
+    out1,
+    send_sem,
+    recv_sem,
+):
+    at = place()
+    loads = [
+        pltpu.make_async_copy(source, target, load_sem.at[k])
+        for k, (source, target) in enumerate(
+            ((w_in_hbm, w_in), (w_up_hbm, w_up), (cot_hbm, dyb), (w_down_hbm, w_down))
+        )
+    ]
+    for load in loads:
+        load.start()
+    greet(at)
+    bufs = (core_in, core_sum, (in0, in1, in2), (out0, out1))
+    outs = (o_down, o_up, o_in)
+    streams = [Stream(k, at, t, outs, bufs, send_sem, recv_sem) for k in range(len(STREAMS))]
+    down, up, rest = streams[:3], streams[3:6], streams[6:]
+    block = 256
+    for load in loads:
+        load.wait()
+
+    def forward(i, carry):
+        rows = aligned(i, block)
+        h = jnp.dot(enc[rows, :], w_in[...], preferred_element_type=f32)
+        h0[rows, :] = h
+        r = lax.rsqrt(jnp.mean(h * h, axis=-1, keepdims=True) + 1e-06)
+        rinv[rows, :] = jnp.broadcast_to(r, (block, CH))
+        u_here = (h * r * gain[...]).astype(bf16)
+        u[rows, :] = u_here
+        dy_here = (dyb[rows, :].astype(f32) * scale).astype(bf16)
+        dyb[rows, :] = dy_here
+        for n in range(WIDTH // block):
+            cols = slice(n * block, (n + 1) * block)
+            act = jnp.dot(u_here, w_up[:, cols], preferred_element_type=f32)
+            back = nt_dot(dy_here, w_down[cols, :])
+            square = act * act
+            tanh = jnp.tanh(TANH_SCALE * act * (1.0 + CUBIC * square))
+            cdf = 0.5 + 0.5 * tanh
+            slope = cdf + act * (0.5 - 0.5 * tanh * tanh) * (
+                TANH_SCALE + (3.0 * CUBIC * TANH_SCALE) * square
+            )
+            g[rows, cols] = (act * cdf).astype(bf16)
+            dact[rows, cols] = (slope * back).astype(bf16)
+        return carry
+
+    lax.fori_loop(0, CELLS // block, forward, 0)
+
+    def weight_grad(left, right, first):
+        def body(i, carry):
+            cols = aligned(i, block)
+            part = tn_dot(left[:, cols], right[...]).astype(bf16)
+            t[0, cols, first : first + 512] = part[:, :512]
+            t[1, cols, first : first + 512] = part[:, 512:]
+            return carry
+
+        lax.fori_loop(0, WIDTH // block, body, 0)
+
+    weight_grad(g, dyb, 0)
+    for s in down:
+        s.core_scatter()
+    weight_grad(u, dact, 512)
+    for s in up:
+        s.core_scatter()
+    for s in down:
+        s.core_add()
+        s.axis_scatter(0)
+
+    gain_sum[...] = jnp.zeros_like(gain_sum)
+
+    def backward(i, carry):
+        rows = aligned(i, block)
+        du = nt_dot(dact[rows, :], w_up[...])
+        h = h0[rows, :]
+        r = rinv[rows, :1]
+        gain_sum[...] += jnp.sum(du * h * r, axis=0, keepdims=True)
+        scaled = du * gain[...]
+        mean = jnp.mean(scaled * h, axis=-1, keepdims=True)
+        dh = (r * scaled - h * (r * r * r * mean) + dyb[rows, :].astype(f32)).astype(bf16)
+        u[rows, :] = dh
+        denc = nt_dot(dh, w_in[...])
+        eight = pl.ds(pl.multiple_of(i * 8, 8), 8)
+        ds[eight] = denc.reshape(8, SIDE, CH) * inv[eight]
+        return carry
+
+    lax.fori_loop(0, CELLS // block, backward, 0)
+    for s in up:
+        s.core_add()
+        s.axis_scatter(0)
+
+    def in_grad(i, carry):
+        cols = aligned(i, block)
+        t[0, cols, 1024:] = tn_dot(u[:, cols], enc[...]).astype(bf16)
+        t[1, cols, 1024:] = jnp.zeros((block, CH), bf16)
+        return carry
+
+    lax.fori_loop(0, WIDTH // block, in_grad, 0)
+    for s in rest:
+        s.core_scatter()
+    for s in down:
+        s.axis_add(0)
+        s.axis_scatter(1)
+
+    for k in (0, 1, 34, 35):
+        dz[k] = jnp.zeros((64, CH), f32)
+
+    def filter_grad(p, sums):
+        here = ds[p]
+        dz[p + 2, :16] = jnp.zeros((16, CH), f32)
+        dz[p + 2, 16:48] = here
+        dz[p + 2, 48:] = jnp.zeros((16, CH), f32)
+        value = enc32[p]
+        new = []
+        for j, (a, b) in enumerate(offsets):
+            near = pad[p + 1 + a, 8 + b : 40 + b, :CH]
+            near_count = pad[p + 1 + a, 8 + b : 40 + b, 2 * CH :]
+            part = here * (near - value * near_count)
+            new.append(sums[j] + jnp.sum(part.reshape(4, 8, CH), axis=0))
+        return tuple(new)
+
+    zeros = jnp.zeros((8, CH), f32)
+    filter_sums = lax.fori_loop(0, SIDE, filter_grad, (zeros,) * 9)
+
+    def bias_grad(p, total):
+        spread = jnp.zeros((48, CH), f32)
+        for j, (a, b) in enumerate(offsets):
+            spread = spread + kern[j : j + 1, :] * dz[p + 1 - a, 8 - b : 56 - b, :]
+        return total + lax.dot_general(
+            pad[p, :, CH : 2 * CH],
+            spread,
+            (((0,), (0,)), ((), ())),
+            precision=lax.Precision.HIGHEST,
+            preferred_element_type=f32,
+        )
+
+    bias_sum = lax.fori_loop(0, 34, bias_grad, jnp.zeros((CH, CH), f32))
+    small = jnp.concatenate(
+        [gain_sum[:, k * CH : (k + 1) * CH] for k in range(8)]
+        + [jnp.sum(part, axis=0, keepdims=True) for part in filter_sums]
+        + [jnp.zeros((7, CH), f32), bias_sum[:16]],
+        axis=0,
+    )
+    small_copies = small_reduce(at, "x", 0, small, boxes, small_send, small_recv)
+    all_small = list(small_copies)
+    for s in rest:
+        s.core_add()
+        s.axis_scatter(0)
+    for s in up:
+        s.axis_add(0)
+        s.axis_scatter(1)
+    for s in down:
+        s.axis_add(1)
+        s.axis_scatter(2)
+
+    def forecast(i, carry):
+        rows = aligned(i, block)
+        y = h0[rows, :] + jnp.dot(g[rows, :], w_down[...], preferred_element_type=f32)
+        dact[rows, :] = y.astype(bf16)
+        return carry
+
+    lax.fori_loop(0, CELLS // block, forecast, 0)
+    store = pltpu.make_async_copy(dact, y_hbm, load_sem.at[4])
+    store.start()
+    for s in down:
+        s.axis_add(2)
+        s.axis_gather(2)
+    for s in rest:
+        s.axis_add(0)
+        s.axis_scatter(1)
+    for s in up:
+        s.axis_add(1)
+        s.axis_scatter(2)
+    small = small_total("x", 0, boxes, small_copies)
+    small_copies = small_reduce(at, "y", 1, small, boxes, small_send, small_recv)
+    all_small += small_copies
+    for s in down:
+        s.gather_wait()
+        s.axis_gather(1)
+    for s in rest:
+        s.axis_add(1)
+        s.axis_scatter(2)
+    for s in up:
+        s.axis_add(2)
+        s.axis_gather(2)
+    small = small_total("y", 1, boxes, small_copies)
+    small_copies = small_reduce(at, "z", 2, small, boxes, small_send, small_recv)
+    all_small += small_copies
+    for s in down:
+        s.gather_wait()
+        s.axis_gather(0)
+    for s in rest:
+        s.axis_add(2)
+        s.axis_gather(2)
+    for s in up:
+        s.gather_wait()
+        s.axis_gather(1)
+    small = small_total("z", 2, boxes, small_copies)
+    small_copies = small_reduce(at, "core", 3, small, boxes, small_send, small_recv)
+    all_small += small_copies
+    for s in rest:
+        s.gather_wait()
+        s.axis_gather(1)
+    for s in up:
+        s.gather_wait()
+        s.axis_gather(0)
+    for s in down:
+        s.gather_wait()
+        s.core_gather()
+    for s in rest:
+        s.gather_wait()
+        s.axis_gather(0)
+    o_small[...] = small_total("core", 3, boxes, small_copies)
+    for s in up + rest:
+        s.gather_wait()
+        s.core_gather()
+    for s in streams:
+        s.finish()
+    for copy in all_small:
+        copy.wait_send()
+    store.wait()
+
+
+def train(scale, enc, enc32, inv, pad, kern, gain, w_in, w_up, w_down, cot):
+    vmem, hbm = pl.BlockSpec(memory_space=pltpu.VMEM), pl.BlockSpec(memory_space=pl.ANY)
+    return pl.pallas_call(
+        functools.partial(train_kernel, scale),
+        out_shape=(
+            jax.ShapeDtypeStruct((CELLS, WIDTH), bf16),
+            jax.ShapeDtypeStruct((WIDTH, WIDTH), bf16),
+            jax.ShapeDtypeStruct((WIDTH, WIDTH), bf16),
+            jax.ShapeDtypeStruct((WIDTH, 2 * CH), bf16),
+            jax.ShapeDtypeStruct((40, CH), f32),
+        ),
+        in_specs=[vmem] * 6 + [hbm] * 4,
+        out_specs=[hbm] + [vmem] * 4,
+        scratch_shapes=[
+            pltpu.VMEM((CH, WIDTH), bf16),
+            pltpu.VMEM((WIDTH, WIDTH), bf16),
+            pltpu.VMEM((WIDTH, WIDTH), bf16),
+            pltpu.VMEM((CELLS, WIDTH), bf16),
+            pltpu.VMEM((CELLS, WIDTH), f32),
+            pltpu.VMEM((CELLS, CH), f32),
+            pltpu.VMEM((CELLS, WIDTH), bf16),
+            pltpu.VMEM((CELLS, WIDTH), bf16),
+            pltpu.VMEM((CELLS, WIDTH), bf16),
+            pltpu.VMEM((SIDE, SIDE, CH), f32),
+            pltpu.VMEM((36, 64, CH), f32),
+            pltpu.VMEM((1, WIDTH), f32),
+            pltpu.VMEM((4, 4, 40, CH), f32),
+            pltpu.VMEM((2, ROWS, HALF), bf16),
+            pltpu.SemaphoreType.DMA((5,)),
+            pltpu.SemaphoreType.DMA((12,)),
+            pltpu.SemaphoreType.DMA((12,)),
+        ]
+        + reduce_scratch(),
+        compiler_params=pltpu.CompilerParams(
+            collective_id=0, has_side_effects=True, vmem_limit_bytes=60 << 20
+        ),
+    )(enc, enc32, inv, pad, kern, gain, w_in, w_up, w_down, cot)
+
+
+def widen_kernel(y, down, up, into, y_out, down_out, up_out, in_out):
+    y_out[...] = y[...]
+    down_out[...] = down[...].astype(f32)
+    up_out[...] = up[...].astype(f32)
+    in_out[...] = into[:, :CH].astype(f32).T
+
+
+def widen(y, down, up, into):
+    block = 128
+    wide = pl.BlockSpec((block, WIDTH), lambda i: (i, 0))
+    return pl.pallas_call(
+        widen_kernel,
+        grid=(WIDTH // block,),
+        out_shape=(
+            jax.ShapeDtypeStruct((CELLS, WIDTH), bf16),
+            jax.ShapeDtypeStruct((WIDTH, WIDTH), f32),
+            jax.ShapeDtypeStruct((WIDTH, WIDTH), f32),
+            jax.ShapeDtypeStruct((CH, WIDTH), f32),
+        ),
+        in_specs=[wide, wide, wide, pl.BlockSpec((block, 2 * CH), lambda i: (i, 0))],
+        out_specs=[wide, wide, wide, pl.BlockSpec((CH, block), lambda i: (0, i))],
+        compiler_params=pltpu.CompilerParams(vmem_limit_bytes=32 << 20),
+    )(y, down, up, into)
+
+
 def shards(
     obs_values,
     obs_instrument,
@@ -554,65 +841,33 @@
     w_down,
     cotangent,
 ):
-    n_inst = lax.axis_size("inst")
-    n_tile = lax.axis_size("tile")
-    channels = obs_values.shape[1]
-    lat_rows, lon_cols, width = cotangent.shape
-    cells = lat_rows * lon_cols
-    instruments = inst_bias.shape[0]
-    enc, enc32, inv, padded = exchange(
+    enc, enc32, inv, pad = exchange(
         obs_values, obs_instrument, obs_target, obs_cell, inst_bias, kernel
     )
-    psums, pkinds = padded[:, 7:41, :channels], padded[:, 7:41, channels : channels + instruments]
-    pcounts = jnp.sum(pkinds, axis=2, keepdims=True)
-
-    def shifted(padded, a, b):
-        return padded[1 + a : 1 + a + lat_rows, 1 + b : 1 + b + lon_cols]
-
-    h0 = jnp.dot(enc, w_in, preferred_element_type=f32)
-    rinv = lax.rsqrt(jnp.mean(h0 * h0, axis=-1, keepdims=True) + 1e-06)
-    normed = (h0 * rinv * norm_gain).astype(bf16)
-    act = jnp.dot(normed, w_up, preferred_element_type=f32)
-    gelu_out, gelu_back = jax.vjp(jax.nn.gelu, act)
-    hidden = gelu_out.astype(bf16)
-    predicted_field = (
-        (h0 + jnp.dot(hidden, w_down, preferred_element_type=f32))
-        .astype(bf16)
-        .reshape(lat_rows, lon_cols, width)
+    scale = 1.0 / (CELLS * DEVICES) ** 0.5
+    y, down, up, into, small = train(
+        scale,
+        enc,
+        enc32,
+        inv,
+        pad,
+        kernel,
+        norm_gain.reshape(1, WIDTH),
+        w_in,
+        w_up,
+        w_down,
+        cotangent.reshape(CELLS, WIDTH),
     )
-    scale = 1.0 / (lat_rows * n_tile * lon_cols * n_inst) ** 0.5
-    dyb = (cotangent.astype(f32) * scale).astype(bf16).reshape(cells, width)
-    gw_down = inner(hidden, dyb)
-    dact = gelu_back(along(dyb, w_down))[0].astype(bf16)
-    gw_up = inner(normed, dact)
-    dnormed = along(dact, w_up)
-    g_gain = jnp.sum(dnormed * h0 * rinv, axis=0)
-    scaled = dnormed * norm_gain
-    dh = (
-        rinv * scaled
-        - h0 * rinv**3 * jnp.mean(scaled * h0, axis=-1, keepdims=True)
-        + dyb.astype(f32)
-    ).astype(bf16)
-    gw_in_t = inner(dh, enc)
-    denc = along(dh, w_in).reshape(lat_rows, lon_cols, channels)
-    dspread = denc * inv
-    ddensity = -dspread * enc32
-    kernel_rows = []
-    bias = jnp.zeros((instruments, channels), f32)
-    flat = dspread.reshape(cells, channels)
-    for j, (a, b) in enumerate(offsets):
-        near = shifted(pkinds, a, b)
-        kernel_rows.append(
-            jnp.sum(dspread * shifted(psums, a, b) + ddensity * shifted(pcounts, a, b), axis=(0, 1))
-        )
-        bias = bias + kernel[j] * inner(
-            near.reshape(cells, instruments), flat, lax.Precision.HIGHEST
-        )
-    g_kernel = jnp.stack(kernel_rows)
-    totals = unpack_grads(
-        all_reduce(pack_grads(gw_down, gw_up, gw_in_t, g_gain, g_kernel, bias))
+    y, down, up, into = widen(y, down, up, into)
+    return (
+        y.reshape(cotangent.shape),
+        into,
+        up,
+        down,
+        small[:8].reshape(WIDTH),
+        small[8:17],
+        small[24:40],
     )
-    return (predicted_field, *totals)
 
 
 def solution(mesh):

time: 169 us -> 145 us (0.86)
  Pallas kernels: 101 us -> 133 us
  matrix products: 30.8 us -> 0 us
  other arithmetic: 22.9 us -> 1.38 us
  local copies, waits for them, and re-layouts: 12.7 us -> 9.68 us
    pallas_call x1 -> x2, Pallas kernels: 47.4 us -> 78.7 us  [the longest x1 73.9 us: train(): pl.pallas_call(functools.partial(train_kernel, scale), out_shape=(jax.Sha...]
    dot_general x18 -> x0, matrix products: 30.8 us -> none  [the longest x12 15.5 us: inner(): lax.dot_general(left, right, (((0,), (0,)), ((), ())), precision=precisio...]
    convert_element_type x6 -> x0, other arithmetic: 13.1 us -> none  [the longest x1 4.2 us: unpack_grads(): jnp.concatenate([o[0, :, :512], o[1, :, :512]], axis=1).astype(f32)]
    another operation x2 -> x0, other arithmetic: 4.7 us -> none  [pack_grads(): return jnp.stack(halves).astype(bf16)]
    squeeze x1 -> x0, local copies, waits for them, and re-layouts: 3.95 us -> none  [unpack_grads(): o[0, :, :512]]
    reduce_sum x3 -> x0, other arithmetic: 3.7 us -> none  [the longest x2 2.26 us: shards(): jnp.sum(dspread * shifted(psums, a, b) + ddensity * shifted(pcounts, a, b...]
    unnamed x21 -> x8, local copies, waits for them, and re-layouts: 3.09 us -> 5.81 us
    slice x4 -> x2, local copies, waits for them, and re-layouts: 3.81 us -> 2.59 us  [the longest x1 1.29 us: shards(): small[24:40]]
where the time goes in v1:
time: 145 us
  Pallas kernels  133 us (92%)
  local copies, waits for them, and re-layouts  9.68 us (7%)
    pallas_call x1, Pallas kernels, train(): pl.pallas_call(functools.partial(train_kernel, scale), out_shape=(jax.Sha...  73.9 us
    pallas_call x1, Pallas kernels, exchange(): pl.pallas_call(exchange_kernel, out_shape=(jax.ShapeDtypeStruct((cells, C...  54.3 us
    unnamed x8, local copies, waits for them, and re-layouts  5.81 us
    pallas_call x1, Pallas kernels, widen(): pl.pallas_call(widen_kernel, grid=(WIDTH // block,), out_shape=(jax.Shape...  4.81 us

profile of v1, /device:TPU:1, one launch (start us, length us, event | category | flops | bytes accessed | tf_op | source)
XLA Modules:
  0.0 144.7 jit_solution(6440911486364640547)
XLA Ops:
  0.6 0.8 fusion.1
  1.4 0.6 pad_maximum_fusion.bias3
  2.0 54.3 %shard_map.162 = (bf16[1024,128]{1,0:T(8,128)(2,1)}, f32[32,32,128]{2,1,0:T(8,128)}, f32[32,32,128]{2,1,0:T(8,128)}, f32[34,48,384]{2,1,0:T(8,128)}) custom-call(bf16[2048,128]{1,0:T(8,128)(2,1)} %values.1, s32[1,2048]{1,0:T(1,128)} %bitcast.9, s32[1,2048]{1,0:T(1,128)} %bitcast.10, s32[1,2048]{1,0:T(1,128)} %bitcast.11, ...), custom_call_target="tpu_custom_call" | custom-call | tf_op jit(solution)/shard_map/pallas_call | solution.py:435
  56.3 73.9 %shard_map.163 = (bf16[1024,1024]{1,0:T(8,128)(2,1)}, bf16[1024,1024]{1,0:T(8,128)(2,1)}, bf16[1024,1024]{1,0:T(8,128)(2,1)}, bf16[1024,256]{1,0:T(8,128)(2,1)}, f32[40,128]{1,0:T(8,128)}) custom-call(bf16[1024,128]{1,0:T(8,128)(2,1)} %get-tuple-element.20.enc, f32[32,32,128]{2,1,0:T(8,128)} %get-tuple-element.21.enc32, ...), custom_call_target="tpu_custom_call" | custom-call | tf_op jit(solution)/shard_map/pallas_call | solution.py:769
  130.2 1.3 slice_bitcast_fusion
  131.5 1.3 slice.11
  132.8 1.3 slice.10
  134.1 0.0 copy-start
  134.1 1.6 %copy-done = bf16[1024,1024]{1,0:T(8,128)(2,1)S(1)} copy-done((bf16[1024,1024]{1,0:T(8,128)(2,1)S(1)}, bf16[1024,1024]{1,0:T(8,128)(2,1)}, u32[]{:S(2)}) %copy-start) | copy-done | bytes 2097176
  135.6 0.0 copy-start.1
  135.6 1.6 %copy-done.1 = bf16[1024,1024]{1,0:T(8,128)(2,1)S(1)} copy-done((bf16[1024,1024]{1,0:T(8,128)(2,1)S(1)}, bf16[1024,1024]{1,0:T(8,128)(2,1)}, u32[]{:S(2)}) %copy-start.1) | copy-done | bytes 2097176
  137.2 0.0 copy-start.2
  137.2 1.6 %copy-done.2 = bf16[1024,1024]{1,0:T(8,128)(2,1)S(1)} copy-done((bf16[1024,1024]{1,0:T(8,128)(2,1)S(1)}, bf16[1024,1024]{1,0:T(8,128)(2,1)}, u32[]{:S(2)}) %copy-start.2) | copy-done | bytes 2097176
  138.8 0.0 copy-start.3
  138.8 1.0 copy-done.3
  139.9 4.8 %shard_map.164 = (bf16[1024,1024]{1,0:T(8,128)(2,1)}, f32[1024,1024]{1,0:T(8,128)}, f32[1024,1024]{1,0:T(8,128)}, f32[128,1024]{1,0:T(8,128)}) custom-call(bf16[1024,1024]{1,0:T(8,128)(2,1)S(1)} %copy-done, bf16[1024,1024]{1,0:T(8,128)(2,1)S(1)} %copy-done.1, bf16[1024,1024]{1,0:T(8,128)(2,1)S(1)} %copy-done.2, bf16[1024,256]{1,0:T(8,128)(2,1)S(1)} %copy-done.3), custom_call_target="tpu_custom_call" | custom-call | tf_op jit(solution)/shard_map/pallas_call | solution.py:816
Async XLA Ops:
  134.1 1.6 %copy-start = (bf16[1024,1024]{1,0:T(8,128)(2,1)S(1)}, bf16[1024,1024]{1,0:T(8,128)(2,1)}, u32[]{:S(2)}) copy-start(bf16[1024,1024]{1,0:T(8,128)(2,1)} %get-tuple-element.24.y) | copy-start | bytes 6291460
  135.6 1.6 %copy-start.1 = (bf16[1024,1024]{1,0:T(8,128)(2,1)S(1)}, bf16[1024,1024]{1,0:T(8,128)(2,1)}, u32[]{:S(2)}) copy-start(bf16[1024,1024]{1,0:T(8,128)(2,1)} %get-tuple-element.25.down) | copy-start | bytes 6291460
  137.2 1.6 %copy-start.2 = (bf16[1024,1024]{1,0:T(8,128)(2,1)S(1)}, bf16[1024,1024]{1,0:T(8,128)(2,1)}, u32[]{:S(2)}) copy-start(bf16[1024,1024]{1,0:T(8,128)(2,1)} %get-tuple-element.26.up) | copy-start | bytes 6291460
  138.8 1.0 copy-start.3

commit v2 on v0

v2 whole, which is shorter than its diff:
```python
import functools

import jax
import jax.numpy as jnp
from jax import lax
from jax.experimental import pallas as pl
from jax.experimental.pallas import tpu as pltpu
from jax.sharding import PartitionSpec as P

offsets = [(a, b) for a in (-1, 0, 1) for b in (-1, 0, 1)]
f32, bf16 = jnp.float32, jnp.bfloat16


MESH = pl.DeviceIdType.MESH
HALF = 1152
ROWS = 1024
STREAMS = (
    (0, 256, ("x", "y", "z"), 0, 0),
    (256, 128, ("y", "z", "x"), 0, 256),
    (384, 128, ("z", "x", "y"), 0, 384),
    (512, 128, ("x", "y", "z"), 1, 0),
    (640, 256, ("y", "z", "x"), 1, 128),
    (896, 128, ("z", "x", "y"), 1, 384),
    (1024, 128, ("z", "x", "y"), 2, 0),
)


def place():
    inst, tile = lax.axis_index("inst"), lax.axis_index("tile")
    return {"z": inst // 4, "x": inst % 4, "y": tile // 2, "core": tile % 2}


def device_at(at):
    return (at["z"] * 4 + at["x"], at["y"] * 2 + at["core"])


def moved(at, axis, step):
    size = 2 if axis == "core" else 4
    return {**at, axis: lax.rem(at[axis] + step, size)}


def send_to(source, landing, send_sem, recv_sem, to):
    copy = pltpu.make_async_remote_copy(
        src_ref=source,
        dst_ref=landing,
        send_sem=send_sem,
        recv_sem=recv_sem,
        device_id=to,
        device_id_type=MESH,
    )
    copy.start()
    return copy


def aligned(index, size):
    return pl.ds(pl.multiple_of(index * size, size), size)


class Stream:
    def __init__(self, number, at, give, keep, outs, bufs, send_sem, recv_sem):
        first, wide, self.order, output, first_out = STREAMS[number]
        self.cols = pl.ds(first, wide)
        self.at, self.give, self.keep, self.o = at, give, keep, outs[output]
        half = self.o.shape[1] // 2
        self.out_cols = pl.ds(pl.multiple_of(at["core"] * half + first_out, 128), wide)
        self.core_in, self.core_sum, self.ins, self.outs = bufs
        self.sends, self.recvs = send_sem.at[number], recv_sem.at[number]
        self.started = []

    def go(self, source, target, slot, at):
        copy = send_to(
            source, target, self.sends.at[slot], self.recvs.at[slot], device_at(at)
        )
        self.started.append(copy)
        return copy

    def core_scatter(self):
        other = moved(self.at, "core", 1)
        self.pending = [
            self.go(self.give.at[:, self.cols], self.core_in.at[:, self.cols], 0, other)
        ]

    def core_add(self):
        for copy in self.pending:
            copy.wait_recv()
        step = 128

        def body(i, carry):
            rows = aligned(i, step)
            total = self.keep[rows, self.cols].astype(f32) + self.core_in[rows, self.cols].astype(f32)
            self.core_sum[rows, self.cols] = total.astype(bf16)
            return carry

        lax.fori_loop(0, ROWS // step, body, 0)

    def axis_scatter(self, level):
        axis, size = self.order[level], (256, 64, 16)[level]
        source = self.core_sum if level == 0 else self.outs[level - 1]
        self.pending = []
        for step in (1, 2, 3):
            peer = moved(self.at, axis, step)
            self.pending.append(
                self.go(
                    source.at[aligned(peer[axis], size), self.cols],
                    self.ins[level].at[step - 1, :, self.cols],
                    1 + 3 * level + step - 1,
                    peer,
                )
            )

    def axis_add(self, level):
        axis, size = self.order[level], (256, 64, 16)[level]
        source = self.core_sum if level == 0 else self.outs[level - 1]
        for copy in self.pending:
            copy.wait_recv()
        step = min(size, 64)

        def body(i, carry):
            rows = aligned(i, step)
            mine = pl.ds(pl.multiple_of(self.at[axis] * size + i * step, step), step)
            total = source[mine, self.cols].astype(f32)
            for j in range(3):
                total = total + self.ins[level][j, rows, self.cols].astype(f32)
            if level < 2:
                self.outs[level][rows, self.cols] = total.astype(bf16)
            else:
                self.o[self.owned(2), self.out_cols] = total.astype(bf16)
            return carry

        lax.fori_loop(0, size // step, body, 0)

    def owned(self, level):
        start = 0
        for axis, size in list(zip(self.order, (256, 64, 16)))[: level + 1]:
            start = start + self.at[axis] * size
        size = (256, 64, 16)[level]
        return pl.ds(pl.multiple_of(start, size), size)

    def axis_gather(self, level):
        axis = self.order[level]
        rows = self.owned(level)
        self.pending = []
        for step in (1, 2, 3):
            peer = moved(self.at, axis, step)
            part = self.o.at[rows, self.out_cols]
            self.pending.append(self.go(part, part, 10 + 3 * (2 - level) + step - 1, peer))

    def gather_wait(self):
        for copy in self.pending:
            copy.wait_recv()

    def core_gather(self):
        part = self.o.at[:, self.out_cols]
        self.pending = [self.go(part, part, 19, moved(self.at, "core", 1))]

    def finish(self):
        self.gather_wait()
        for copy in self.started:
            copy.wait_send()


def reduce_scratch():
    return [
        pltpu.VMEM((ROWS, HALF), bf16),
        pltpu.VMEM((ROWS, HALF), bf16),
        pltpu.VMEM((3, 256, HALF), bf16),
        pltpu.VMEM((3, 64, HALF), bf16),
        pltpu.VMEM((3, 16, HALF), bf16),
        pltpu.VMEM((256, HALF), bf16),
        pltpu.VMEM((64, HALF), bf16),
        pltpu.SemaphoreType.DMA((len(STREAMS), 20)),
        pltpu.SemaphoreType.DMA((len(STREAMS), 20)),
    ]


DEVICES, SLOTS, CH = 128, 32, 128
SIDE = 32
OBS_HERE = 2048


def iota(shape, axis):
    return lax.broadcasted_iota(jnp.int32, shape, axis)


def nt_dot(left, right):
    return lax.dot_general(left, right, (((1,), (1,)), ((), ())), preferred_element_type=f32)


def tn_dot(left, right):
    return lax.dot_general(left, right, (((0,), (0,)), ((), ())), preferred_element_type=f32)


WIDTH = 1024
CELLS = SIDE * SIDE
TANH_SCALE = 0.7978845608028654
CUBIC = 0.044715
SCALE = 1.0 / (CELLS * DEVICES) ** 0.5


def small_reduce(at, axis, level, mine, boxes, send_sem, recv_sem):
    size = 2 if axis == "core" else 4
    boxes[level, at[axis]] = mine
    copies = []
    for step in range(1, size):
        box = boxes.at[level, at[axis]]
        k = 3 * level + step - 1
        copies.append(
            send_to(box, box, send_sem.at[k], recv_sem.at[k], device_at(moved(at, axis, step)))
        )
    return copies


def small_total(axis, level, boxes, copies):
    for copy in copies:
        copy.wait_recv()
    total = boxes[level, 0]
    for k in range(1, 2 if axis == "core" else 4):
        total = total + boxes[level, k]
    return total


def counts_of(kinds):
    shape = kinds.shape
    flat = kinds.reshape(-1, CH)
    lane = iota(flat.shape, 1)
    return jnp.where(lane < 16, pltpu.roll(flat, CH // 2, 1), flat).reshape(shape)


def step_kernel(
    values,
    instr,
    target,
    cell,
    bias,
    kern,
    gain,
    w_in_hbm,
    w_up_hbm,
    w_down_hbm,
    cot_hbm,
    y_hbm,
    down_hbm,
    up_hbm,
    in_hbm,
    o_small,
    feat,
    places,
    packed,
    tags_out,
    got,
    tags_in,
    lands,
    right,
    spots,
    pad,
    side_out,
    side_in,
    corner_out,
    corner_in,
    sems,
    halo_send,
    halo_recv,
    o_down,
    o_up,
    o_in,
    enc,
    enc32,
    inv,
    w_in,
    w_up,
    w_down,
    dyb,
    back,
    h0,
    rinv,
    u,
    dact,
    ds,
    dz,
    two,
    gain_sum,
    boxes,
    load_sem,
    small_send,
    small_recv,
    core_in,
    core_sum,
    in0,
    in1,
    in2,
    out0,
    out1,
    send_sem,
    recv_sem,
):
    at = place()
    inst, tile = lax.axis_index("inst"), lax.axis_index("tile")
    me = inst * 8 + tile
    barrier = pltpu.get_barrier_semaphore()
    loads = [
        pltpu.make_async_copy(source, landing, load_sem.at[k])
        for k, (source, landing) in enumerate(
            ((cot_hbm, dyb), (w_down_hbm, w_down), (w_in_hbm, w_in), (w_up_hbm, w_up))
        )
    ]
    for load in loads:
        load.start()

    def greet_one(i, carry):
        peer = lax.rem(me + i, DEVICES)
        pl.semaphore_signal(
            barrier, inc=1, device_id=(peer // 8, lax.rem(peer, 8)), device_id_type=MESH
        )
        return carry

    lax.fori_loop(1, DEVICES, greet_one, 0)

    def clear(p, carry):
        pad[p] = jnp.zeros((48, 2 * CH), f32)
        dz[p] = jnp.zeros((64, CH), f32)
        return carry

    lax.fori_loop(0, 34, clear, 0)
    for k in (34, 35):
        dz[k] = jnp.zeros((64, CH), f32)

    block = 256
    upper = (iota((block, block), 0) < iota((block, block), 1)).astype(bf16)
    ahead = jnp.zeros((DEVICES, 1), f32)
    tags = jnp.zeros((DEVICES, CH), f32)
    for b in range(OBS_HERE // block):
        cols = slice(b * block, (b + 1) * block)
        to = target[:, cols]
        hit = (to == iota((DEVICES, block), 0)).astype(f32)
        hit16 = hit.astype(bf16)
        before = jnp.dot(hit16, upper, preferred_element_type=f32) + ahead
        slot = jnp.sum(hit * before, axis=0, keepdims=True)
        ahead = ahead + jnp.sum(hit, axis=1, keepdims=True)
        slot = slot.astype(jnp.int32)
        places[:, cols] = to * SLOTS + slot
        mine = (slot == iota((SLOTS, block), 0)).astype(f32)
        where = cell[:, cols]
        notes = jnp.concatenate(
            [
                mine * (where // SIDE + 1).astype(f32),
                mine * (where % SIDE + 1).astype(f32),
                mine * (instr[:, cols] + 1).astype(f32),
                jnp.zeros((SLOTS, block), f32),
            ],
            axis=0,
        ).astype(bf16)
        tags = tags + nt_dot(hit16, notes)
    for t in range(DEVICES):
        tags_out[t] = tags[t : t + 1, :]

    pl.semaphore_wait(barrier, DEVICES - 1)

    def send_slot(source, landing, k, to_inst, to_tile):
        t = to_inst * 8 + to_tile
        pltpu.make_async_remote_copy(
            src_ref=source.at[t],
            dst_ref=landing.at[me],
            send_sem=sems.at[k],
            recv_sem=sems.at[2 + k],
            device_id=(to_inst, to_tile),
            device_id_type=MESH,
        ).start()

    def send_tags(i, carry):
        peer = lax.rem(me + i * 37, DEVICES)
        send_slot(tags_out, tags_in, 1, peer // 8, lax.rem(peer, 8))
        return carry

    lax.fori_loop(1, DEVICES, send_tags, 0)

    hi = bias[...].astype(bf16)
    rest_part = bias[...] - hi.astype(f32)
    mid = rest_part.astype(bf16)
    low = (rest_part - mid.astype(f32)).astype(bf16)
    bias3 = jnp.concatenate([hi, mid, low], axis=0)
    for b in range(OBS_HERE // block):
        cols = slice(b * block, (b + 1) * block)
        pick = (instr[:, cols] == iota((16, block), 0)).astype(f32)
        pick3 = jnp.concatenate([pick, pick, pick], axis=0).T.astype(bf16)
        offset = jnp.dot(pick3, bias3, preferred_element_type=f32)
        feat[cols, :] = (values[cols, :].astype(f32) + offset).astype(bf16)

    group = 8 * SLOTS

    def pack_and_send(i, carry):
        turn = lax.rem(i * 7, 16)
        to_inst = lax.rem(at["z"] + turn // 4, 4) * 4 + lax.rem(at["x"] + lax.rem(turn, 4), 4)
        spot = jnp.clip(places[...] - to_inst * group, -1, group).astype(f32).astype(bf16)
        number = iota((group, OBS_HERE), 0).astype(f32).astype(bf16)
        choose = jnp.where(spot == number, jnp.bfloat16(1), jnp.bfloat16(0))
        rows = jnp.dot(choose, feat[...], preferred_element_type=f32).astype(bf16)
        packed[pl.ds(pl.multiple_of(to_inst * 8, 8), 8)] = rows.reshape(8, SLOTS, CH)

        def send_one(j, inner_carry):
            to_tile = lax.rem(tile + j * 3, 8)

            @pl.when(to_inst * 8 + to_tile != me)
            def _():
                send_slot(packed, got, 0, to_inst, to_tile)

            return inner_carry

        lax.fori_loop(0, 8, send_one, 0)
        return carry

    lax.fori_loop(1, 17, pack_and_send, 0)
    got[me] = packed[me]
    tags_in[me] = tags_out[me]
    others = pl.ds(0, DEVICES - 1)
    pltpu.make_async_copy(tags_in.at[others], tags_in.at[others], sems.at[3]).wait()
    every = tags_in[...].reshape(DEVICES, CH)
    for k in range(3):
        spots[k] = jnp.concatenate(
            [every[SIDE * m : SIDE * (m + 1), 32 * k : 32 * (k + 1)] for m in range(4)], axis=1
        )

    def place_group(g, carry):
        row = pl.ds(g, 1)
        lat, lon, kind = (spots[k, row, :] for k in range(3))
        number = iota((SIDE, CH), 0).astype(f32) + 1.0
        at_lon = (lon == number).astype(f32)
        cols = aligned(g, CH)
        for p in range(SIDE):
            lands[p * SIDE : (p + 1) * SIDE, cols] = jnp.where(
                lat == float(p + 1), at_lon, 0.0
            ).astype(bf16)
        which = iota((CH, CH), 0)
        kinds = jnp.where(
            which < 16, (kind == which.astype(f32) + 1.0).astype(f32), (kind > 0.0).astype(f32)
        )
        right[cols, CH:] = kinds.T.astype(bf16)
        return carry

    lax.fori_loop(0, SIDE, place_group, 0)

    half = CELLS // 2

    def go_back(i):
        rows = pl.ds(i * half, half)
        dy_here = (dyb[rows, :].astype(f32) * SCALE).astype(bf16)
        dyb[rows, :] = dy_here
        back[rows, :] = nt_dot(dy_here, w_down[...])

    loads[0].wait()
    loads[1].wait()
    go_back(0)
    pltpu.make_async_copy(got.at[others], got.at[others], sems.at[2]).wait()

    def collect_rows(g, carry):
        for m in range(4):
            rows = pl.ds(pl.multiple_of(g * CH + m * SLOTS, SLOTS), SLOTS)
            right[rows, :CH] = got[g + SIDE * m]
        return carry

    lax.fori_loop(0, SIDE, collect_rows, 0)

    def sum_block(i, carry):
        total = jnp.dot(lands[aligned(i, half), :], right[...], preferred_element_type=f32)
        pad[pl.ds(1 + 16 * i, 16), 8:40, :] = total.reshape(16, SIDE, 2 * CH)
        return carry

    lax.fori_loop(0, 2, sum_block, 0)

    for p in range(SIDE):
        side_out[0, p : p + 1, :] = pad[1 + p, 8:9, :]
        side_out[1, p : p + 1, :] = pad[1 + p, 39:40, :]
    for k, (p, q) in enumerate(((1, 8), (1, 39), (32, 8), (32, 39))):
        corner_out[k] = pad[p, q : q + 1, :]
    north, south = lax.rem(tile + 7, 8), lax.rem(tile + 1, 8)
    west, east = lax.rem(inst + 15, 16), lax.rem(inst + 1, 16)
    halo = (
        (pad.at[1, 8:40], pad.at[33, 8:40], (inst, north)),
        (pad.at[32, 8:40], pad.at[0, 8:40], (inst, south)),
        (side_out.at[0], side_in.at[1], (west, tile)),
        (side_out.at[1], side_in.at[0], (east, tile)),
        (corner_out.at[0], corner_in.at[3], (west, north)),
        (corner_out.at[1], corner_in.at[2], (east, north)),
        (corner_out.at[2], corner_in.at[1], (west, south)),
        (corner_out.at[3], corner_in.at[0], (east, south)),
    )
    halo_copies = [
        send_to(source, landing, halo_send.at[k], halo_recv.at[k], to)
        for k, (source, landing, to) in enumerate(halo)
    ]
    go_back(1)
    for load in loads[2:]:
        load.wait()
    for copy in halo_copies:
        copy.wait_recv()
    keep_north = (tile > 0).astype(f32)
    keep_south = (tile < 7).astype(f32)
    keep_west = (inst > 0).astype(f32)
    keep_east = (inst < 15).astype(f32)
    pad[0, 8:40, :] = pad[0, 8:40, :] * keep_north
    pad[33, 8:40, :] = pad[33, 8:40, :] * keep_south
    for p in range(SIDE):
        pad[1 + p, 7:8, :] = side_in[0, p : p + 1, :] * keep_west
        pad[1 + p, 40:41, :] = side_in[1, p : p + 1, :] * keep_east
    pad[0, 7:8, :] = corner_in[0] * (keep_north * keep_west)
    pad[0, 40:41, :] = corner_in[1] * (keep_north * keep_east)
    pad[33, 7:8, :] = corner_in[2] * (keep_south * keep_west)
    pad[33, 40:41, :] = corner_in[3] * (keep_south * keep_east)

    lats = 4

    def encode(i, carry):
        spread = jnp.zeros((lats, SIDE, CH), f32)
        density = jnp.zeros((lats, SIDE, CH), f32)
        near = pl.ds(lats * i, lats + 2)
        for b in (-1, 0, 1):
            sums = pad[near, 8 + b : 40 + b, :CH]
            counts = counts_of(pad[near, 8 + b : 40 + b, CH:])
            for a in (-1, 0, 1):
                j = 3 * (a + 1) + (b + 1)
                weight = kern[j : j + 1, :].reshape(1, 1, CH)
                spread = spread + weight * sums[1 + a : 1 + a + lats]
                density = density + weight * counts[1 + a : 1 + a + lats]
        share = 1.0 / (1.0 + density)
        value = spread * share
        here = pl.ds(lats * i, lats)
        inv[here] = share
        enc32[here] = value
        enc[aligned(i, lats * SIDE), :] = value.reshape(lats * SIDE, CH).astype(bf16)
        return carry

    lax.fori_loop(0, SIDE // lats, encode, 0)
    for copy in halo_copies:
        copy.wait_send()
    for source, k in ((packed, 0), (tags_out, 1)):
        pltpu.make_async_copy(source.at[others], source.at[others], sems.at[k]).wait()

    give, keep = lands.at[:, :HALF], lands.at[:, HALF : 2 * HALF]
    g = lands.at[:, 2 * HALF : 2 * HALF + WIDTH]
    bufs = (core_in, core_sum, (in0, in1, in2), (out0, out1))
    outs = (o_down, o_up, o_in)
    streams = [
        Stream(k, at, give, keep, outs, bufs, send_sem, recv_sem) for k in range(len(STREAMS))
    ]
    down, up, rest = [streams[k] for k in (1, 2, 0)], [streams[k] for k in (3, 5, 4)], streams[6:]
    core = at["core"]

    def forward(i, carry):
        rows = aligned(i, block)
        h = jnp.dot(enc[rows, :], w_in[...], preferred_element_type=f32)
        h0[rows, :] = h
        r = lax.rsqrt(jnp.mean(h * h, axis=-1, keepdims=True) + 1e-06)
        rinv[rows, :] = jnp.broadcast_to(r, (block, CH))
        u_here = (h * r * gain[...]).astype(bf16)
        u[rows, :] = u_here
        for n in range(WIDTH // block):
            cols = slice(n * block, (n + 1) * block)
            act = jnp.dot(u_here, w_up[:, cols], preferred_element_type=f32)
            square = act * act
            tanh = jnp.tanh(TANH_SCALE * act * (1.0 + CUBIC * square))
            cdf = 0.5 + 0.5 * tanh
            slope = cdf + act * (0.5 - 0.5 * tanh * tanh) * (
                TANH_SCALE + (3.0 * CUBIC * TANH_SCALE) * square
            )
            g[rows, cols] = (act * cdf).astype(bf16)
            dact[rows, cols] = (slope * back[rows, cols]).astype(bf16)
        return carry

    lax.fori_loop(0, CELLS // block, forward, 0)

    def weight_grad(left, right_side, into, part, first):
        cols_in = aligned(part, 512)

        def body(i, carry):
            cols = aligned(i, 512)
            into[cols, first : first + 512] = tn_dot(left[:, cols], right_side[:, cols_in]).astype(
                bf16
            )
            return carry

        lax.fori_loop(0, WIDTH // 512, body, 0)

    weight_grad(g, dyb, give, 1 - core, 0)
    for s in down:
        s.core_scatter()
    weight_grad(g, dyb, keep, core, 0)
    for s in down:
        s.core_add()
        s.axis_scatter(0)
    weight_grad(u, dact, give, 1 - core, 512)
    for s in up:
        s.core_scatter()
    weight_grad(u, dact, keep, core, 512)
    for s in up:
        s.core_add()
        s.axis_scatter(0)

    gain_sum[...] = jnp.zeros_like(gain_sum)

    def backward(i, carry):
        rows = aligned(i, block)
        du = nt_dot(dact[rows, :], w_up[...])
        h = h0[rows, :]
        r = rinv[rows, :1]
        gain_sum[...] += jnp.sum(du * h * r, axis=0, keepdims=True)
        scaled = du * gain[...]
        mean = jnp.mean(scaled * h, axis=-1, keepdims=True)
        dh = (r * scaled - h * (r * r * r * mean) + dyb[rows, :].astype(f32)).astype(bf16)
        u[rows, :] = dh
        denc = nt_dot(dh, w_in[...])
        eight = pl.ds(pl.multiple_of(i * 8, 8), 8)
        ds[eight] = denc.reshape(8, SIDE, CH) * inv[eight]
        return carry

    lax.fori_loop(0, 2, backward, 0)
    for s in down:
        s.axis_add(0)
        s.axis_scatter(1)
    lax.fori_loop(2, 4, backward, 0)
    for s in down:
        s.axis_add(1)
        s.axis_scatter(2)

    def in_grad(i, carry):
        cols = aligned(i, block)
        part = tn_dot(enc[...], u[:, cols]).T
        give[cols, 1024:] = jnp.where(core == 1, part, 0.0).astype(bf16)
        keep[cols, 1024:] = jnp.where(core == 0, part, 0.0).astype(bf16)
        return carry

    lax.fori_loop(0, WIDTH // block, in_grad, 0)
    for s in rest:
        s.core_scatter()
    for s in up:
        s.axis_add(0)
        s.axis_scatter(1)

    def filter_grad(i, totals):
        near, here = pl.ds(lats * i, lats + 2), pl.ds(lats * i, lats)
        slope = ds[here]
        dz[pl.ds(lats * i + 2, lats), 16:48] = slope
        both = slope * enc32[here]
        new = list(totals)
        for b in (-1, 0, 1):
            sums = pad[near, 8 + b : 40 + b, :CH]
            counts = counts_of(pad[near, 8 + b : 40 + b, CH:])
            for a in (-1, 0, 1):
                j = 3 * (a + 1) + (b + 1)
                part = slope * sums[1 + a : 1 + a + lats] - both * counts[1 + a : 1 + a + lats]
                new[j] = new[j] + jnp.sum(part.reshape(lats * 4, 8, CH), axis=0)
        return tuple(new)

    zeros = jnp.zeros((8, CH), f32)
    filter_sums = lax.fori_loop(0, SIDE // lats, filter_grad, (zeros,) * 9)
    for s in down:
        s.axis_add(2)
        s.axis_gather(2)
    for s in rest:
        s.core_add()
        s.axis_scatter(0)

    def spread_back(i, carry):
        value = jnp.zeros((2, 48, CH), f32)
        for b in (-1, 0, 1):
            slab = dz[pl.ds(2 * i, 4), 8 - b : 56 - b, :]
            for a in (-1, 0, 1):
                j = 3 * (a + 1) + (b + 1)
                value = value + kern[j : j + 1, :].reshape(1, 1, CH) * slab[1 - a : 3 - a]
        kinds = pad[pl.ds(2 * i, 2), :, CH:]
        rows = aligned(i, 96)
        for part, k in ((value, 0), (kinds, 1)):
            part = part.reshape(96, CH)
            top = part.astype(bf16)
            two[k, rows, :CH] = top
            two[k, rows, CH:] = (part - top.astype(f32)).astype(bf16)
        return carry

    lax.fori_loop(0, 17, spread_back, 0)
    quarters = tn_dot(two[1], two[0])
    bias_sum = (quarters[:16, :CH] + quarters[:16, CH:]) + (
        quarters[CH : CH + 16, :CH] + quarters[CH : CH + 16, CH:]
    )
    small = jnp.concatenate(
        [gain_sum[:, k * CH : (k + 1) * CH] for k in range(8)]
        + [jnp.sum(part, axis=0, keepdims=True) for part in filter_sums]
        + [jnp.zeros((7, CH), f32), bias_sum],
        axis=0,
    )
    small_copies = small_reduce(at, "x", 0, small, boxes, small_send, small_recv)
    all_small = list(small_copies)
    for s in up:
        s.axis_add(1)
        s.axis_scatter(2)
    for s in down:
        s.gather_wait()
        s.axis_gather(1)

    def forecast(i):
        rows = pl.ds(i * half, half)
        y = h0[rows, :] + jnp.dot(g[rows, :], w_down[...], preferred_element_type=f32)
        dact[rows, :] = y.astype(bf16)

    forecast(0)
    for s in rest:
        s.axis_add(0)
        s.axis_scatter(1)
    small = small_total("x", 0, boxes, small_copies)
    small_copies = small_reduce(at, "y", 1, small, boxes, small_send, small_recv)
    all_small += small_copies
    for s in up:
        s.axis_add(2)
        s.axis_gather(2)
    for s in down:
        s.gather_wait()
        s.axis_gather(0)
    forecast(1)
    stores = [pltpu.make_async_copy(dact, y_hbm, load_sem.at[4])]
    stores[0].start()
    for s in rest:
        s.axis_add(1)
        s.axis_scatter(2)
    small = small_total("y", 1, boxes, small_copies)
    small_copies = small_reduce(at, "z", 2, small, boxes, small_send, small_recv)
    all_small += small_copies
    for s in up:
        s.gather_wait()
        s.axis_gather(1)
    for s in rest:
        s.axis_add(2)
        s.axis_gather(2)
    small = small_total("z", 2, boxes, small_copies)
    small_copies = small_reduce(at, "core", 3, small, boxes, small_send, small_recv)
    all_small += small_copies
    for s in up:
        s.gather_wait()
        s.axis_gather(0)
    for s in rest:
        s.gather_wait()
        s.axis_gather(1)
    for s in down:
        s.gather_wait()
        s.core_gather()
    o_small[...] = small_total("core", 3, boxes, small_copies)
    for s in rest:
        s.gather_wait()
        s.axis_gather(0)
    for s in down:
        s.finish()
    stores.append(pltpu.make_async_copy(o_down, down_hbm, load_sem.at[5]))
    stores[1].start()
    for s in up + rest:
        s.gather_wait()
        s.core_gather()
    for s in up + rest:
        s.finish()
    for k, (source, landing) in enumerate(((o_up, up_hbm), (o_in, in_hbm))):
        stores.append(pltpu.make_async_copy(source, landing, load_sem.at[6 + k]))
        stores[2 + k].start()
    for copy in all_small:
        copy.wait_send()
    for store in stores:
        store.wait()


def step(values, instr, target, cell, bias, kern, gain, w_in, w_up, w_down, cot):
    vmem, hbm = pl.BlockSpec(memory_space=pltpu.VMEM), pl.BlockSpec(memory_space=pl.ANY)
    return pl.pallas_call(
        step_kernel,
        out_shape=(
            jax.ShapeDtypeStruct((CELLS, WIDTH), bf16),
            jax.ShapeDtypeStruct((WIDTH, WIDTH), bf16),
            jax.ShapeDtypeStruct((WIDTH, WIDTH), bf16),
            jax.ShapeDtypeStruct((WIDTH, 2 * CH), bf16),
            jax.ShapeDtypeStruct((40, CH), f32),
        ),
        in_specs=[vmem] * 7 + [hbm] * 4,
        out_specs=[hbm] * 4 + [vmem],
        scratch_shapes=[
            pltpu.VMEM((OBS_HERE, CH), bf16),
            pltpu.VMEM((1, OBS_HERE), jnp.int32),
            pltpu.VMEM((DEVICES, SLOTS, CH), bf16),
            pltpu.VMEM((DEVICES, 1, CH), f32),
            pltpu.VMEM((DEVICES, SLOTS, CH), bf16),
            pltpu.VMEM((DEVICES, 1, CH), f32),
            pltpu.VMEM((CELLS, DEVICES * SLOTS), bf16),
            pltpu.VMEM((DEVICES * SLOTS, 2 * CH), bf16),
            pltpu.VMEM((3, SIDE, CH), f32),
            pltpu.VMEM((34, 48, 2 * CH), f32),
            pltpu.VMEM((2, SIDE, 2 * CH), f32),
            pltpu.VMEM((2, SIDE, 2 * CH), f32),
            pltpu.VMEM((4, 1, 2 * CH), f32),
            pltpu.VMEM((4, 1, 2 * CH), f32),
            pltpu.SemaphoreType.DMA((4,)),
            pltpu.SemaphoreType.DMA((8,)),
            pltpu.SemaphoreType.DMA((8,)),
            pltpu.VMEM((WIDTH, WIDTH), bf16),
            pltpu.VMEM((WIDTH, WIDTH), bf16),
            pltpu.VMEM((WIDTH, 2 * CH), bf16),
            pltpu.VMEM((CELLS, CH), bf16),
            pltpu.VMEM((SIDE, SIDE, CH), f32),
            pltpu.VMEM((SIDE, SIDE, CH), f32),
            pltpu.VMEM((CH, WIDTH), bf16),
            pltpu.VMEM((WIDTH, WIDTH), bf16),
            pltpu.VMEM((WIDTH, WIDTH), bf16),
            pltpu.VMEM((CELLS, WIDTH), bf16),
            pltpu.VMEM((CELLS, WIDTH), f32),
            pltpu.VMEM((CELLS, WIDTH), f32),
            pltpu.VMEM((CELLS, CH), f32),
            pltpu.VMEM((CELLS, WIDTH), bf16),
            pltpu.VMEM((CELLS, WIDTH), bf16),
            pltpu.VMEM((SIDE, SIDE, CH), f32),
            pltpu.VMEM((36, 64, CH), f32),
            pltpu.VMEM((2, 34 * 48, 2 * CH), bf16),
            pltpu.VMEM((1, WIDTH), f32),
            pltpu.VMEM((4, 4, 40, CH), f32),
            pltpu.SemaphoreType.DMA((8,)),
            pltpu.SemaphoreType.DMA((12,)),
            pltpu.SemaphoreType.DMA((12,)),
        ]
        + reduce_scratch(),
        compiler_params=pltpu.CompilerParams(
            collective_id=0, has_side_effects=True, vmem_limit_bytes=62 << 20
        ),
    )(values, instr, target, cell, bias, kern, gain, w_in, w_up, w_down, cot)


def widen_kernel(y, down, up, into, small, y_out, down_out, up_out, in_out, gain, kern, bias):
    y_out[...] = y[...]
    down_out[...] = down[...].astype(f32)
    up_out[...] = up[...].astype(f32)
    in_out[...] = into[:, :CH].astype(f32).T
    gain[...] = small[:8]
    kern[...] = small[8:17]
    bias[...] = small[24:40]


def widen(y, down, up, into, small):
    block = 128
    wide = pl.BlockSpec((block, WIDTH), lambda i: (i, 0))

    def whole(rows):
        return pl.BlockSpec((rows, CH), lambda i: (0, 0))

    return pl.pallas_call(
        widen_kernel,
        grid=(WIDTH // block,),
        out_shape=(
            jax.ShapeDtypeStruct((CELLS, WIDTH), bf16),
            jax.ShapeDtypeStruct((WIDTH, WIDTH), f32),
            jax.ShapeDtypeStruct((WIDTH, WIDTH), f32),
            jax.ShapeDtypeStruct((CH, WIDTH), f32),
            jax.ShapeDtypeStruct((8, CH), f32),
            jax.ShapeDtypeStruct((9, CH), f32),
            jax.ShapeDtypeStruct((16, CH), f32),
        ),
        in_specs=[wide, wide, wide, pl.BlockSpec((block, 2 * CH), lambda i: (i, 0)), whole(40)],
        out_specs=[
            wide,
            wide,
            wide,
            pl.BlockSpec((CH, block), lambda i: (0, i)),
            whole(8),
            whole(9),
            whole(16),
        ],
        compiler_params=pltpu.CompilerParams(vmem_limit_bytes=60 << 20),
    )(y, down, up, into, small)


def shards(
    obs_values,
    obs_instrument,
    obs_target,
    obs_cell,
    inst_bias,
    kernel,
    w_in,
    norm_gain,
    w_up,
    w_down,
    cotangent,
):
    y, down, up, into, small = step(
        obs_values,
        obs_instrument.reshape(1, OBS_HERE),
        obs_target.reshape(1, OBS_HERE),
        obs_cell.reshape(1, OBS_HERE),
        inst_bias,
        kernel,
        norm_gain.reshape(1, WIDTH),
        w_in,
        w_up,
        w_down,
        cotangent.reshape(CELLS, WIDTH),
    )
    y, down, up, into, gain, filters, bias = widen(y, down, up, into, small)
    return (y.reshape(cotangent.shape), into, up, down, gain.reshape(WIDTH), filters, bias)


def solution(mesh):
    return jax.shard_map(
        shards,
        mesh=mesh,
        in_specs=(
            P(("inst", "tile"), None),
            P(("inst", "tile")),
            P(("inst", "tile"), None),
            P(("inst", "tile")),
            P(),
            P(),
            P(),
            P(),
            P(),
            P(),
            P("tile", "inst", None),
        ),
        out_specs=(P("tile", "inst", None), P(), P(), P(), P(), P(), P()),
        check_vma=False,
    )
```

time: 169 us -> 111 us (0.66)
  matrix products: 30.8 us -> 0 us
  other arithmetic: 22.9 us -> 0 us
  local copies, waits for them, and re-layouts: 12.7 us -> 0 us
  Pallas kernels: 101 us -> 109 us
    dot_general x18 -> x0, matrix products: 30.8 us -> none  [the longest x12 15.5 us: inner(): lax.dot_general(left, right, (((0,), (0,)), ((), ())), precision=precisio...]
    convert_element_type x7 -> x0, other arithmetic: 13.9 us -> none  [the longest x1 4.2 us: unpack_grads(): jnp.concatenate([o[0, :, :512], o[1, :, :512]], axis=1).astype(f32)]
    pallas_call x2, Pallas kernels: 101 us -> 109 us  [the longest x1 101 us: step(): pl.pallas_call(step_kernel, out_shape=(jax.ShapeDtypeStruct((CELLS, WIDTH...]
    another operation x2 -> x0, other arithmetic: 4.7 us -> none  [pack_grads(): return jnp.stack(halves).astype(bf16)]
    squeeze x1 -> x0, local copies, waits for them, and re-layouts: 3.95 us -> none  [unpack_grads(): o[0, :, :512]]
    slice x4 -> x0, local copies, waits for them, and re-layouts: 3.81 us -> none  [the longest x1 1.48 us: pack_grads(): gw_down[:, :512]]
    reduce_sum x3 -> x0, other arithmetic: 3.7 us -> none  [the longest x2 2.26 us: shards(): jnp.sum(dspread * shifted(psums, a, b) + ddensity * shifted(pcounts, a, b...]
    unnamed x21 -> x0, local copies, waits for them, and re-layouts: 3.09 us -> none
where the time goes in v2:
time: 111 us; the launch traced here: 110 us
  Pallas kernels  109 us (98%)
    pallas_call x1, Pallas kernels, step(): pl.pallas_call(step_kernel, out_shape=(jax.ShapeDtypeStruct((CELLS, WIDTH...  101 us
    pallas_call x1, Pallas kernels, widen(): pl.pallas_call(widen_kernel, grid=(WIDTH // block,), out_shape=(jax.Shape...  8.5 us

profile of v2, /device:TPU:1, one launch (start us, length us, event | category | flops | bytes accessed | tf_op | source)
XLA Modules:
  0.0 110.2 jit_solution(17620152720858762254)
XLA Ops:
  0.6 100.9 %shard_map.162 = (bf16[1024,1024]{1,0:T(8,128)(2,1)}, bf16[1024,1024]{1,0:T(8,128)(2,1)}, bf16[1024,1024]{1,0:T(8,128)(2,1)}, bf16[1024,256]{1,0:T(8,128)(2,1)}, f32[40,128]{1,0:T(8,128)}) custom-call(bf16[2048,128]{1,0:T(8,128)(2,1)} %values.1, s32[1,2048]{1,0:T(1,128)} %bitcast.8, s32[1,2048]{1,0:T(1,128)} %bitcast.9, s32[1,2048]{1,0:T(1,128)} %bitcast.10, ...), custom_call_target="tpu_custom_call" | custom-call | tf_op jit(solution)/shard_map/pallas_call | solution.py:766
  101.5 8.5 %shard_map.163 = (bf16[1024,1024]{1,0:T(8,128)(2,1)}, f32[1024,1024]{1,0:T(8,128)}, f32[1024,1024]{1,0:T(8,128)}, f32[128,1024]{1,0:T(8,128)}, f32[8,128]{1,0:T(...) custom-call(bf16[1024,1024]{1,0:T(8,128)(2,1)} %get-tuple-element.19.y, bf16[1024,1024]{1,0:T(8,128)(2,1)} %get-tuple-element.20.down, ...), custom_call_target="tpu_custom_call" | custom-call | tf_op jit(solution)/shard_map/pallas_call | solution.py:843

commit v3 on v2

--- a/solution.py
+++ b/solution.py
@@ -15,13 +15,19 @@
 HALF = 1152
 ROWS = 1024
 STREAMS = (
-    (0, 256, ("x", "y", "z"), 0, 0),
-    (256, 128, ("y", "z", "x"), 0, 256),
-    (384, 128, ("z", "x", "y"), 0, 384),
-    (512, 128, ("x", "y", "z"), 1, 0),
-    (640, 256, ("y", "z", "x"), 1, 128),
-    (896, 128, ("z", "x", "y"), 1, 384),
-    (1024, 128, ("z", "x", "y"), 2, 0),
+    (0, 256, "x", "yz", 0, 0),
+    (256, 256, "y", "zx", 0, 256),
+    (512, 256, "z", "xy", 1, 0),
+    (768, 128, "x", "yz", 1, 256),
+    (896, 128, "y", "zx", 1, 384),
+    (1024, 128, "z", "xy", 2, 0),
+)
+
+
+PLAN = (
+    "gd0", 1, 0, "gd1", "gu0", 2, 4, "gu1", "b0", 0, 3, 2, 4, "b1", 1, "b2", "b3", "i", 5, 4, 0,
+    3, 5, 2, 1, 4, "f", 3, 5, 0, 2, 1, 4, 5, 0, 3, 2, "t", "s", 1, "y0", 5, 3, 4, "s", "y1", 0,
+    "s", 2, 3, 1, "s", 5, 4, 0, "s", 1, 3, 2, 5,
 )
 
 
@@ -58,105 +64,122 @@
 
 class Stream:
     def __init__(self, number, at, give, keep, outs, bufs, send_sem, recv_sem):
-        first, wide, self.order, output, first_out = STREAMS[number]
+        first, wide, self.axis, self.plane, output, first_out = STREAMS[number]
         self.cols = pl.ds(first, wide)
         self.at, self.give, self.keep, self.o = at, give, keep, outs[output]
         half = self.o.shape[1] // 2
         self.out_cols = pl.ds(pl.multiple_of(at["core"] * half + first_out, 128), wide)
-        self.core_in, self.core_sum, self.ins, self.outs = bufs
+        self.core_in, self.core_sum, self.axis_in, self.plane_in, self.axis_sum = bufs
         self.sends, self.recvs = send_sem.at[number], recv_sem.at[number]
-        self.started = []
+        self.mine = at[self.plane[0]] * 4 + at[self.plane[1]]
+        self.done = 0
 
     def go(self, source, target, slot, at):
-        copy = send_to(
-            source, target, self.sends.at[slot], self.recvs.at[slot], device_at(at)
-        )
-        self.started.append(copy)
-        return copy
-
-    def core_scatter(self):
+        send_to(source, target, self.sends.at[slot], self.recvs.at[slot], device_at(at))
+
+    def to_axis(self, slot, refs):
+        for step in (1, 2, 3):
+            peer = moved(self.at, self.axis, step)
+            self.go(*refs(step, peer), slot, peer)
+
+    def to_plane(self, slot, refs):
+        def body(step, carry):
+            peer = moved(self.at, self.plane[0], step // 4)
+            peer = moved(peer, self.plane[1], lax.rem(step, 4))
+            self.go(*refs(step, peer), slot, peer)
+            return carry
+
+        lax.fori_loop(1, 16, body, 0)
+
+    def arrived(self, slot, ref):
+        pltpu.make_async_copy(ref, ref, self.recvs.at[slot]).wait()
+
+    def rows_of(self, count):
+        return self.o.at[pl.ds(0, count), self.out_cols]
+
+    def my_rows(self, size):
+        start = self.at[self.axis] * 256
+        if size == 16:
+            start = start + self.mine * 16
+        return pl.ds(pl.multiple_of(start, size), size)
+
+    def step0(self):
         other = moved(self.at, "core", 1)
-        self.pending = [
-            self.go(self.give.at[:, self.cols], self.core_in.at[:, self.cols], 0, other)
-        ]
-
-    def core_add(self):
-        for copy in self.pending:
-            copy.wait_recv()
-        step = 128
+        self.go(self.give.at[:, self.cols], self.core_in.at[:, self.cols], 0, other)
+
+    def step1(self):
+        self.arrived(0, self.core_in.at[:, self.cols])
+        size = 256
 
         def body(i, carry):
-            rows = aligned(i, step)
+            rows = aligned(i, size)
             total = self.keep[rows, self.cols].astype(f32) + self.core_in[rows, self.cols].astype(f32)
             self.core_sum[rows, self.cols] = total.astype(bf16)
             return carry
 
-        lax.fori_loop(0, ROWS // step, body, 0)
-
-    def axis_scatter(self, level):
-        axis, size = self.order[level], (256, 64, 16)[level]
-        source = self.core_sum if level == 0 else self.outs[level - 1]
-        self.pending = []
-        for step in (1, 2, 3):
-            peer = moved(self.at, axis, step)
-            self.pending.append(
-                self.go(
-                    source.at[aligned(peer[axis], size), self.cols],
-                    self.ins[level].at[step - 1, :, self.cols],
-                    1 + 3 * level + step - 1,
-                    peer,
-                )
-            )
-
-    def axis_add(self, level):
-        axis, size = self.order[level], (256, 64, 16)[level]
-        source = self.core_sum if level == 0 else self.outs[level - 1]
-        for copy in self.pending:
-            copy.wait_recv()
-        step = min(size, 64)
+        lax.fori_loop(0, ROWS // size, body, 0)
+        self.to_axis(
+            1,
+            lambda step, peer: (
+                self.core_sum.at[aligned(peer[self.axis], 256), self.cols],
+                self.axis_in.at[step - 1, :, self.cols],
+            ),
+        )
+
+    def step2(self):
+        self.arrived(1, self.axis_in.at[:, :, self.cols])
+        size = 64
 
         def body(i, carry):
-            rows = aligned(i, step)
-            mine = pl.ds(pl.multiple_of(self.at[axis] * size + i * step, step), step)
-            total = source[mine, self.cols].astype(f32)
+            rows = aligned(i, size)
+            own = pl.ds(pl.multiple_of(self.at[self.axis] * 256 + i * size, size), size)
+            total = self.core_sum[own, self.cols].astype(f32)
             for j in range(3):
-                total = total + self.ins[level][j, rows, self.cols].astype(f32)
-            if level < 2:
-                self.outs[level][rows, self.cols] = total.astype(bf16)
-            else:
-                self.o[self.owned(2), self.out_cols] = total.astype(bf16)
+                total = total + self.axis_in[j, rows, self.cols].astype(f32)
+            self.axis_sum[rows, self.cols] = total.astype(bf16)
             return carry
 
-        lax.fori_loop(0, size // step, body, 0)
-
-    def owned(self, level):
-        start = 0
-        for axis, size in list(zip(self.order, (256, 64, 16)))[: level + 1]:
-            start = start + self.at[axis] * size
-        size = (256, 64, 16)[level]
-        return pl.ds(pl.multiple_of(start, size), size)
-
-    def axis_gather(self, level):
-        axis = self.order[level]
-        rows = self.owned(level)
-        self.pending = []
-        for step in (1, 2, 3):
-            peer = moved(self.at, axis, step)
-            part = self.o.at[rows, self.out_cols]
-            self.pending.append(self.go(part, part, 10 + 3 * (2 - level) + step - 1, peer))
-
-    def gather_wait(self):
-        for copy in self.pending:
-            copy.wait_recv()
-
-    def core_gather(self):
+        lax.fori_loop(0, 256 // size, body, 0)
+        self.to_plane(
+            2,
+            lambda step, peer: (
+                self.axis_sum.at[
+                    aligned(peer[self.plane[0]] * 4 + peer[self.plane[1]], 16), self.cols
+                ],
+                self.plane_in.at[step - 1, :, self.cols],
+            ),
+        )
+
+    def step3(self):
+        self.arrived(2, self.plane_in.at[:, :, self.cols])
+        total = self.axis_sum[aligned(self.mine, 16), self.cols].astype(f32)
+        for j in range(15):
+            total = total + self.plane_in[j, :, self.cols].astype(f32)
+        self.o[self.my_rows(16), self.out_cols] = total.astype(bf16)
+        part = self.o.at[self.my_rows(16), self.out_cols]
+        self.to_plane(3, lambda step, peer: (part, part))
+
+    def step4(self):
+        self.arrived(3, self.rows_of(240))
+        part = self.o.at[self.my_rows(256), self.out_cols]
+        self.to_axis(4, lambda step, peer: (part, part))
+
+    def step5(self):
+        self.arrived(4, self.rows_of(768))
         part = self.o.at[:, self.out_cols]
-        self.pending = [self.go(part, part, 19, moved(self.at, "core", 1))]
+        self.go(part, part, 5, moved(self.at, "core", 1))
+
+    def step6(self):
+        self.arrived(5, self.rows_of(ROWS))
+
+    def advance(self):
+        getattr(self, "step" + str(self.done))()
+        self.done += 1
 
     def finish(self):
-        self.gather_wait()
-        for copy in self.started:
-            copy.wait_send()
+        for slot, rows in enumerate((ROWS, 768, 240, 240, 768, ROWS)):
+            ref = self.rows_of(rows)
+            pltpu.make_async_copy(ref, ref, self.sends.at[slot]).wait()
 
 
 def reduce_scratch():
@@ -164,12 +187,10 @@
         pltpu.VMEM((ROWS, HALF), bf16),
         pltpu.VMEM((ROWS, HALF), bf16),
         pltpu.VMEM((3, 256, HALF), bf16),
-        pltpu.VMEM((3, 64, HALF), bf16),
-        pltpu.VMEM((3, 16, HALF), bf16),
+        pltpu.VMEM((15, 16, HALF), bf16),
         pltpu.VMEM((256, HALF), bf16),
-        pltpu.VMEM((64, HALF), bf16),
-        pltpu.SemaphoreType.DMA((len(STREAMS), 20)),
-        pltpu.SemaphoreType.DMA((len(STREAMS), 20)),
+        pltpu.SemaphoreType.DMA((len(STREAMS), 6)),
+        pltpu.SemaphoreType.DMA((len(STREAMS), 6)),
     ]
 
 
@@ -260,6 +281,7 @@
     sems,
     halo_send,
     halo_recv,
+    rows_in,
     o_down,
     o_up,
     o_in,
@@ -287,9 +309,7 @@
     core_sum,
     in0,
     in1,
-    in2,
     out0,
-    out1,
     send_sem,
     recv_sem,
 ):
@@ -306,14 +326,23 @@
     for load in loads:
         load.start()
 
-    def greet_one(i, carry):
-        peer = lax.rem(me + i, DEVICES)
-        pl.semaphore_signal(
-            barrier, inc=1, device_id=(peer // 8, lax.rem(peer, 8)), device_id_type=MESH
-        )
-        return carry
-
-    lax.fori_loop(1, DEVICES, greet_one, 0)
+    def greet_row(i, carry):
+        peer = (inst, lax.rem(tile + i, 8))
+        pl.semaphore_signal(barrier, inc=1, device_id=peer, device_id_type=MESH)
+        return carry
+
+    def greet_column(i, carry):
+        peer = (lax.rem(inst + i, 16), tile)
+        pl.semaphore_signal(barrier, inc=1, device_id=peer, device_id_type=MESH)
+        return carry
+
+    def tell_column(i, carry):
+        peer = (lax.rem(inst + i, 16), tile)
+        pl.semaphore_signal(rows_in, inc=1, device_id=peer, device_id_type=MESH)
+        return carry
+
+    lax.fori_loop(1, 8, greet_row, 0)
+    lax.fori_loop(1, 16, greet_column, 0)
 
     def clear(p, carry):
         pad[p] = jnp.zeros((48, 2 * CH), f32)
@@ -353,25 +382,8 @@
     for t in range(DEVICES):
         tags_out[t] = tags[t : t + 1, :]
 
-    pl.semaphore_wait(barrier, DEVICES - 1)
-
-    def send_slot(source, landing, k, to_inst, to_tile):
-        t = to_inst * 8 + to_tile
-        pltpu.make_async_remote_copy(
-            src_ref=source.at[t],
-            dst_ref=landing.at[me],
-            send_sem=sems.at[k],
-            recv_sem=sems.at[2 + k],
-            device_id=(to_inst, to_tile),
-            device_id_type=MESH,
-        ).start()
-
-    def send_tags(i, carry):
-        peer = lax.rem(me + i * 37, DEVICES)
-        send_slot(tags_out, tags_in, 1, peer // 8, lax.rem(peer, 8))
-        return carry
-
-    lax.fori_loop(1, DEVICES, send_tags, 0)
+    pl.semaphore_wait(barrier, 22)
+    lax.fori_loop(1, 16, tell_column, 0)
 
     hi = bias[...].astype(bf16)
     rest_part = bias[...] - hi.astype(f32)
@@ -385,6 +397,24 @@
         offset = jnp.dot(pick3, bias3, preferred_element_type=f32)
         feat[cols, :] = (values[cols, :].astype(f32) + offset).astype(bf16)
 
+    pl.semaphore_wait(rows_in, 15)
+
+    def send_slot(source, landing, k, to_inst, to_tile):
+        t = to_inst * 8 + to_tile
+        pltpu.make_async_remote_copy(
+            src_ref=source.at[t],
+            dst_ref=landing.at[me],
+            send_sem=sems.at[k],
+            recv_sem=sems.at[2 + k],
+            device_id=(to_inst, to_tile),
+            device_id_type=MESH,
+        ).start()
+
+    def send_tags(i, carry):
+        peer = lax.rem(me + i * 37, DEVICES)
+        send_slot(tags_out, tags_in, 1, peer // 8, lax.rem(peer, 8))
+        return carry
+
     group = 8 * SLOTS
 
     def pack_and_send(i, carry):
@@ -406,6 +436,9 @@
             return inner_carry
 
         lax.fori_loop(0, 8, send_one, 0)
+        lax.fori_loop(
+            jnp.minimum((i - 1) * 16 + 1, DEVICES), jnp.minimum(i * 16 + 1, DEVICES), send_tags, 0
+        )
         return carry
 
     lax.fori_loop(1, 17, pack_and_send, 0)
@@ -536,12 +569,11 @@
 
     give, keep = lands.at[:, :HALF], lands.at[:, HALF : 2 * HALF]
     g = lands.at[:, 2 * HALF : 2 * HALF + WIDTH]
-    bufs = (core_in, core_sum, (in0, in1, in2), (out0, out1))
+    bufs = (core_in, core_sum, in0, in1, out0)
     outs = (o_down, o_up, o_in)
     streams = [
         Stream(k, at, give, keep, outs, bufs, send_sem, recv_sem) for k in range(len(STREAMS))
     ]
-    down, up, rest = [streams[k] for k in (1, 2, 0)], [streams[k] for k in (3, 5, 4)], streams[6:]
     core = at["core"]
 
     def forward(i, carry):
@@ -579,25 +611,10 @@
 
         lax.fori_loop(0, WIDTH // 512, body, 0)
 
-    weight_grad(g, dyb, give, 1 - core, 0)
-    for s in down:
-        s.core_scatter()
-    weight_grad(g, dyb, keep, core, 0)
-    for s in down:
-        s.core_add()
-        s.axis_scatter(0)
-    weight_grad(u, dact, give, 1 - core, 512)
-    for s in up:
-        s.core_scatter()
-    weight_grad(u, dact, keep, core, 512)
-    for s in up:
-        s.core_add()
-        s.axis_scatter(0)
-
     gain_sum[...] = jnp.zeros_like(gain_sum)
 
     def backward(i, carry):
-        rows = aligned(i, block)
+        rows = pl.ds(i * block, block)
         du = nt_dot(dact[rows, :], w_up[...])
         h = h0[rows, :]
         r = rinv[rows, :1]
@@ -607,18 +624,9 @@
         dh = (r * scaled - h * (r * r * r * mean) + dyb[rows, :].astype(f32)).astype(bf16)
         u[rows, :] = dh
         denc = nt_dot(dh, w_in[...])
-        eight = pl.ds(pl.multiple_of(i * 8, 8), 8)
+        eight = pl.ds(i * 8, 8)
         ds[eight] = denc.reshape(8, SIDE, CH) * inv[eight]
         return carry
-
-    lax.fori_loop(0, 2, backward, 0)
-    for s in down:
-        s.axis_add(0)
-        s.axis_scatter(1)
-    lax.fori_loop(2, 4, backward, 0)
-    for s in down:
-        s.axis_add(1)
-        s.axis_scatter(2)
 
     def in_grad(i, carry):
         cols = aligned(i, block)
@@ -626,13 +634,6 @@
         give[cols, 1024:] = jnp.where(core == 1, part, 0.0).astype(bf16)
         keep[cols, 1024:] = jnp.where(core == 0, part, 0.0).astype(bf16)
         return carry
-
-    lax.fori_loop(0, WIDTH // block, in_grad, 0)
-    for s in rest:
-        s.core_scatter()
-    for s in up:
-        s.axis_add(0)
-        s.axis_scatter(1)
 
     def filter_grad(i, totals):
         near, here = pl.ds(lats * i, lats + 2), pl.ds(lats * i, lats)
@@ -649,15 +650,6 @@
                 new[j] = new[j] + jnp.sum(part.reshape(lats * 4, 8, CH), axis=0)
         return tuple(new)
 
-    zeros = jnp.zeros((8, CH), f32)
-    filter_sums = lax.fori_loop(0, SIDE // lats, filter_grad, (zeros,) * 9)
-    for s in down:
-        s.axis_add(2)
-        s.axis_gather(2)
-    for s in rest:
-        s.core_add()
-        s.axis_scatter(0)
-
     def spread_back(i, carry):
         value = jnp.zeros((2, 48, CH), f32)
         for b in (-1, 0, 1):
@@ -674,91 +666,89 @@
             two[k, rows, CH:] = (part - top.astype(f32)).astype(bf16)
         return carry
 
-    lax.fori_loop(0, 17, spread_back, 0)
-    quarters = tn_dot(two[1], two[0])
-    bias_sum = (quarters[:16, :CH] + quarters[:16, CH:]) + (
-        quarters[CH : CH + 16, :CH] + quarters[CH : CH + 16, CH:]
-    )
-    small = jnp.concatenate(
-        [gain_sum[:, k * CH : (k + 1) * CH] for k in range(8)]
-        + [jnp.sum(part, axis=0, keepdims=True) for part in filter_sums]
-        + [jnp.zeros((7, CH), f32), bias_sum],
-        axis=0,
-    )
-    small_copies = small_reduce(at, "x", 0, small, boxes, small_send, small_recv)
-    all_small = list(small_copies)
-    for s in up:
-        s.axis_add(1)
-        s.axis_scatter(2)
-    for s in down:
-        s.gather_wait()
-        s.axis_gather(1)
-
     def forecast(i):
         rows = pl.ds(i * half, half)
         y = h0[rows, :] + jnp.dot(g[rows, :], w_down[...], preferred_element_type=f32)
         dact[rows, :] = y.astype(bf16)
 
-    forecast(0)
-    for s in rest:
-        s.axis_add(0)
-        s.axis_scatter(1)
-    small = small_total("x", 0, boxes, small_copies)
-    small_copies = small_reduce(at, "y", 1, small, boxes, small_send, small_recv)
-    all_small += small_copies
-    for s in up:
-        s.axis_add(2)
-        s.axis_gather(2)
-    for s in down:
-        s.gather_wait()
-        s.axis_gather(0)
-    forecast(1)
-    stores = [pltpu.make_async_copy(dact, y_hbm, load_sem.at[4])]
-    stores[0].start()
-    for s in rest:
-        s.axis_add(1)
-        s.axis_scatter(2)
-    small = small_total("y", 1, boxes, small_copies)
-    small_copies = small_reduce(at, "z", 2, small, boxes, small_send, small_recv)
-    all_small += small_copies
-    for s in up:
-        s.gather_wait()
-        s.axis_gather(1)
-    for s in rest:
-        s.axis_add(2)
-        s.axis_gather(2)
-    small = small_total("z", 2, boxes, small_copies)
-    small_copies = small_reduce(at, "core", 3, small, boxes, small_send, small_recv)
-    all_small += small_copies
-    for s in up:
-        s.gather_wait()
-        s.axis_gather(0)
-    for s in rest:
-        s.gather_wait()
-        s.axis_gather(1)
-    for s in down:
-        s.gather_wait()
-        s.core_gather()
-    o_small[...] = small_total("core", 3, boxes, small_copies)
-    for s in rest:
-        s.gather_wait()
-        s.axis_gather(0)
-    for s in down:
+    totals = {}
+
+    def take_filter():
+        zeros = jnp.zeros((8, CH), f32)
+        totals["filter"] = lax.fori_loop(0, SIDE // lats, filter_grad, (zeros,) * 9)
+
+    def take_small():
+        lax.fori_loop(0, 17, spread_back, 0)
+        quarters = tn_dot(two[1], two[0])
+        bias_sum = (quarters[:16, :CH] + quarters[:16, CH:]) + (
+            quarters[CH : CH + 16, :CH] + quarters[CH : CH + 16, CH:]
+        )
+        totals["small"] = jnp.concatenate(
+            [gain_sum[:, k * CH : (k + 1) * CH] for k in range(8)]
+            + [jnp.sum(part, axis=0, keepdims=True) for part in totals["filter"]]
+            + [jnp.zeros((7, CH), f32), bias_sum],
+            axis=0,
+        )
+
+    all_small, small_levels = [], ("x", "y", "z", "core")
+
+    def pass_small():
+        level = totals.get("level", 0)
+        if level:
+            total = small_total(small_levels[level - 1], level - 1, boxes, totals["copies"])
+        else:
+            total = totals["small"]
+        if level == 4:
+            o_small[...] = total
+            return
+        totals["copies"] = small_reduce(
+            at, small_levels[level], level, total, boxes, small_send, small_recv
+        )
+        all_small.extend(totals["copies"])
+        totals["level"] = level + 1
+
+    stores = []
+
+    def store(source, landing):
+        stores.append(pltpu.make_async_copy(source, landing, load_sem.at[4 + len(stores)]))
+        stores[-1].start()
+
+    def last_forecast():
+        forecast(1)
+        store(dact, y_hbm)
+
+    tasks = {
+        "gd0": lambda: weight_grad(g, dyb, give, 1 - core, 0),
+        "gd1": lambda: weight_grad(g, dyb, keep, core, 0),
+        "gu0": lambda: weight_grad(u, dact, give, 1 - core, 512),
+        "gu1": lambda: weight_grad(u, dact, keep, core, 512),
+        "b0": lambda: backward(0, 0),
+        "b1": lambda: backward(1, 0),
+        "b2": lambda: backward(2, 0),
+        "b3": lambda: backward(3, 0),
+        "i": lambda: lax.fori_loop(0, WIDTH // block, in_grad, 0),
+        "f": take_filter,
+        "t": take_small,
+        "s": pass_small,
+        "y0": lambda: forecast(0),
+        "y1": last_forecast,
+    }
+    for task in PLAN:
+        if task in tasks:
+            tasks[task]()
+            continue
+        streams[task].advance()
+        if streams[0].done == 7 and streams[1].done == 7 and task in (0, 1):
+            store(o_down, down_hbm)
+        if all(streams[k].done == 7 for k in (2, 3, 4)) and task in (2, 3, 4):
+            store(o_up, up_hbm)
+    store(o_in, in_hbm)
+    for s in streams:
         s.finish()
-    stores.append(pltpu.make_async_copy(o_down, down_hbm, load_sem.at[5]))
-    stores[1].start()
-    for s in up + rest:
-        s.gather_wait()
-        s.core_gather()
-    for s in up + rest:
-        s.finish()
-    for k, (source, landing) in enumerate(((o_up, up_hbm), (o_in, in_hbm))):
-        stores.append(pltpu.make_async_copy(source, landing, load_sem.at[6 + k]))
-        stores[2 + k].start()
     for copy in all_small:
         copy.wait_send()
-    for store in stores:
-        store.wait()
+    for copy in stores:
+        copy.wait()
 
 
 def step(values, instr, target, cell, bias, kern, gain, w_in, w_up, w_down, cot):
@@ -792,6 +782,7 @@
             pltpu.SemaphoreType.DMA((4,)),
             pltpu.SemaphoreType.DMA((8,)),
             pltpu.SemaphoreType.DMA((8,)),
+            pltpu.SemaphoreType.REGULAR,
             pltpu.VMEM((WIDTH, WIDTH), bf16),
             pltpu.VMEM((WIDTH, WIDTH), bf16),
             pltpu.VMEM((WIDTH, 2 * CH), bf16),
@@ -823,26 +814,52 @@
     )(values, instr, target, cell, bias, kern, gain, w_in, w_up, w_down, cot)
 
 
-def widen_kernel(y, down, up, into, small, y_out, down_out, up_out, in_out, gain, kern, bias):
-    y_out[...] = y[...]
-    down_out[...] = down[...].astype(f32)
-    up_out[...] = up[...].astype(f32)
-    in_out[...] = into[:, :CH].astype(f32).T
+def widen_kernel(
+    y, down, up, into, small, y_out, down_out, up_out, in_out, gain, kern, bias, *scratch
+):
+    down_in, up_in, in_in, down_wide, up_wide, in_wide, sems, out_sems = scratch
+    size, parts = 256, 4
+    rows = [pl.ds(k * size, size) for k in range(parts)]
+    loads = [pltpu.make_async_copy(into, in_in, sems.at[0])]
+    for k in range(parts):
+        for which, (source, landing) in enumerate(((down, down_in), (up, up_in))):
+            loads.append(
+                pltpu.make_async_copy(
+                    source.at[rows[k]], landing.at[rows[k]], sems.at[1 + 2 * k + which]
+                )
+            )
+    for load in loads:
+        load.start()
+    stores = [pltpu.make_async_copy(y, y_out, out_sems.at[0])]
+    stores[0].start()
     gain[...] = small[:8]
     kern[...] = small[8:17]
     bias[...] = small[24:40]
+    loads[0].wait()
+    for k in range(parts):
+        in_wide[:, k * size : (k + 1) * size] = in_in[rows[k], :CH].astype(f32).T
+    stores.append(pltpu.make_async_copy(in_wide, in_out, out_sems.at[1]))
+    stores[1].start()
+    for k in range(parts):
+        for which, (narrow, wide, landing) in enumerate(
+            ((down_in, down_wide, down_out), (up_in, up_wide, up_out))
+        ):
+            loads[1 + 2 * k + which].wait()
+            wide[rows[k], :] = narrow[rows[k], :].astype(f32)
+            stores.append(
+                pltpu.make_async_copy(
+                    wide.at[rows[k]], landing.at[rows[k]], out_sems.at[2 + 2 * k + which]
+                )
+            )
+            stores[-1].start()
+    for store in stores:
+        store.wait()
 
 
 def widen(y, down, up, into, small):
-    block = 128
-    wide = pl.BlockSpec((block, WIDTH), lambda i: (i, 0))
-
-    def whole(rows):
-        return pl.BlockSpec((rows, CH), lambda i: (0, 0))
-
+    vmem, hbm = pl.BlockSpec(memory_space=pltpu.VMEM), pl.BlockSpec(memory_space=pl.ANY)
     return pl.pallas_call(
         widen_kernel,
-        grid=(WIDTH // block,),
         out_shape=(
             jax.ShapeDtypeStruct((CELLS, WIDTH), bf16),
             jax.ShapeDtypeStruct((WIDTH, WIDTH), f32),
@@ -852,15 +869,17 @@
             jax.ShapeDtypeStruct((9, CH), f32),
             jax.ShapeDtypeStruct((16, CH), f32),
         ),
-        in_specs=[wide, wide, wide, pl.BlockSpec((block, 2 * CH), lambda i: (i, 0)), whole(40)],
-        out_specs=[
-            wide,
-            wide,
-            wide,
-            pl.BlockSpec((CH, block), lambda i: (0, i)),
-            whole(8),
-            whole(9),
-            whole(16),
+        in_specs=[hbm] * 4 + [vmem],
+        out_specs=[hbm] * 4 + [vmem] * 3,
+        scratch_shapes=[
+            pltpu.VMEM((WIDTH, WIDTH), bf16),
+            pltpu.VMEM((WIDTH, WIDTH), bf16),
+            pltpu.VMEM((WIDTH, 2 * CH), bf16),
+            pltpu.VMEM((WIDTH, WIDTH), f32),
+            pltpu.VMEM((WIDTH, WIDTH), f32),
+            pltpu.VMEM((CH, WIDTH), f32),
+            pltpu.SemaphoreType.DMA((9,)),
+            pltpu.SemaphoreType.DMA((10,)),
         ],
         compiler_params=pltpu.CompilerParams(vmem_limit_bytes=60 << 20),
     )(y, down, up, into, small)

time: 111 us -> 169 us (1.52)
  Pallas kernels: 109 us -> 168 us
    pallas_call x1, Pallas kernels: 8.5 us -> 66.2 us  [widen(): pl.pallas_call(widen_kernel, out_shape=(jax.ShapeDtypeStruct((CELLS, WIDT...]
where the time goes in v3:
time: 169 us; the launch traced here: 168 us
  Pallas kernels  168 us (99%)
    pallas_call x1, Pallas kernels, step(): pl.pallas_call(step_kernel, out_shape=(jax.ShapeDtypeStruct((CELLS, WIDTH...  101 us
    pallas_call x1, Pallas kernels, widen(): pl.pallas_call(widen_kernel, out_shape=(jax.ShapeDtypeStruct((CELLS, WIDT...  66.2 us

profile of v3, /device:TPU:1, one launch (start us, length us, event | category | flops | bytes accessed | tf_op | source)
XLA Modules:
  0.0 168.3 jit_solution(6192957150219093442)
XLA Ops:
  0.6 101.4 %shard_map.162 = (bf16[1024,1024]{1,0:T(8,128)(2,1)}, bf16[1024,1024]{1,0:T(8,128)(2,1)}, bf16[1024,1024]{1,0:T(8,128)(2,1)}, bf16[1024,256]{1,0:T(8,128)(2,1)}, f32[40,128]{1,0:T(8,128)}) custom-call(bf16[2048,128]{1,0:T(8,128)(2,1)} %values.1, s32[1,2048]{1,0:T(1,128)} %bitcast.8, s32[1,2048]{1,0:T(1,128)} %bitcast.9, s32[1,2048]{1,0:T(1,128)} %bitcast.10, ...), custom_call_target="tpu_custom_call" | custom-call | tf_op jit(solution)/shard_map/pallas_call | solution.py:756
  102.0 66.2 %shard_map.163 = (bf16[1024,1024]{1,0:T(8,128)(2,1)}, f32[1024,1024]{1,0:T(8,128)}, f32[1024,1024]{1,0:T(8,128)}, f32[128,1024]{1,0:T(8,128)}, f32[8,128]{1,0:T(...) custom-call(bf16[1024,1024]{1,0:T(8,128)(2,1)} %get-tuple-element.19.y, bf16[1024,1024]{1,0:T(8,128)(2,1)} %get-tuple-element.20.down, ...), custom_call_target="tpu_custom_call" | custom-call | tf_op jit(solution)/shard_map/pallas_call | solution.py:861

commit v4 on v3

--- a/solution.py
+++ b/solution.py
@@ -25,9 +25,9 @@
 
 
 PLAN = (
-    "gd0", 1, 0, "gd1", "gu0", 2, 4, "gu1", "b0", 0, 3, 2, 4, "b1", 1, "b2", "b3", "i", 5, 4, 0,
-    3, 5, 2, 1, 4, "f", 3, 5, 0, 2, 1, 4, 5, 0, 3, 2, "t", "s", 1, "y0", 5, 3, 4, "s", "y1", 0,
-    "s", 2, 3, 1, "s", 5, 4, 0, "s", 1, 3, 2, 5,
+    "gd0", 0, 1, "gd1", 0, 1, "gu0", 2, 3, 4, "gu1", 2, 3, 4, "b0", "b1", "b2", "b3", 0, 1, "i",
+    5, 2, 3, 4, 5, "f", 0, 1, "t", "s", 2, 3, 4, 5, "s", 0, 1, "y0", 2, 3, 4, 5, "s", "y1", 0,
+    1, 2, 3, 4, 5, "s", 0, 1, 2, 3, 4, 5, "s", 5,
 )
 
 
@@ -817,38 +817,38 @@
 def widen_kernel(
     y, down, up, into, small, y_out, down_out, up_out, in_out, gain, kern, bias, *scratch
 ):
-    down_in, up_in, in_in, down_wide, up_wide, in_wide, sems, out_sems = scratch
+    y_in, down_in, up_in, in_in, down_wide, up_wide, in_wide, sems, out_sems = scratch
     size, parts = 256, 4
     rows = [pl.ds(k * size, size) for k in range(parts)]
     loads = [pltpu.make_async_copy(into, in_in, sems.at[0])]
     for k in range(parts):
-        for which, (source, landing) in enumerate(((down, down_in), (up, up_in))):
+        for which, (source, landing) in enumerate(((down, down_in), (up, up_in), (y, y_in))):
             loads.append(
                 pltpu.make_async_copy(
-                    source.at[rows[k]], landing.at[rows[k]], sems.at[1 + 2 * k + which]
+                    source.at[rows[k]], landing.at[rows[k]], sems.at[1 + 3 * k + which]
                 )
             )
     for load in loads:
         load.start()
-    stores = [pltpu.make_async_copy(y, y_out, out_sems.at[0])]
-    stores[0].start()
+    stores = []
     gain[...] = small[:8]
     kern[...] = small[8:17]
     bias[...] = small[24:40]
     loads[0].wait()
     for k in range(parts):
         in_wide[:, k * size : (k + 1) * size] = in_in[rows[k], :CH].astype(f32).T
-    stores.append(pltpu.make_async_copy(in_wide, in_out, out_sems.at[1]))
-    stores[1].start()
+    stores.append(pltpu.make_async_copy(in_wide, in_out, out_sems.at[0]))
+    stores[0].start()
     for k in range(parts):
         for which, (narrow, wide, landing) in enumerate(
-            ((down_in, down_wide, down_out), (up_in, up_wide, up_out))
+            ((down_in, down_wide, down_out), (up_in, up_wide, up_out), (y_in, y_in, y_out))
         ):
-            loads[1 + 2 * k + which].wait()
-            wide[rows[k], :] = narrow[rows[k], :].astype(f32)
+            loads[1 + 3 * k + which].wait()
+            if which < 2:
+                wide[rows[k], :] = narrow[rows[k], :].astype(f32)
             stores.append(
                 pltpu.make_async_copy(
-                    wide.at[rows[k]], landing.at[rows[k]], out_sems.at[2 + 2 * k + which]
+                    wide.at[rows[k]], landing.at[rows[k]], out_sems.at[1 + 3 * k + which]
                 )
             )
             stores[-1].start()
@@ -872,14 +872,15 @@
         in_specs=[hbm] * 4 + [vmem],
         out_specs=[hbm] * 4 + [vmem] * 3,
         scratch_shapes=[
+            pltpu.VMEM((CELLS, WIDTH), bf16),
             pltpu.VMEM((WIDTH, WIDTH), bf16),
             pltpu.VMEM((WIDTH, WIDTH), bf16),
             pltpu.VMEM((WIDTH, 2 * CH), bf16),
             pltpu.VMEM((WIDTH, WIDTH), f32),
             pltpu.VMEM((WIDTH, WIDTH), f32),
             pltpu.VMEM((CH, WIDTH), f32),
-            pltpu.SemaphoreType.DMA((9,)),
-            pltpu.SemaphoreType.DMA((10,)),
+            pltpu.SemaphoreType.DMA((13,)),
+            pltpu.SemaphoreType.DMA((13,)),
         ],
         compiler_params=pltpu.CompilerParams(vmem_limit_bytes=60 << 20),
     )(y, down, up, into, small)

time: 169 us -> 107 us (0.63)
  Pallas kernels: 168 us -> 106 us
    pallas_call x1, Pallas kernels: 66.2 us -> 7.33 us  [widen(): pl.pallas_call(widen_kernel, out_shape=(jax.ShapeDtypeStruct((CELLS, WIDT...]
    pallas_call x1, Pallas kernels: 101 us -> 98.6 us  [step(): pl.pallas_call(step_kernel, out_shape=(jax.ShapeDtypeStruct((CELLS, WIDTH...]
where the time goes in v4:
time: 107 us
  Pallas kernels  106 us (99%)
    pallas_call x1, Pallas kernels, step(): pl.pallas_call(step_kernel, out_shape=(jax.ShapeDtypeStruct((CELLS, WIDTH...  98.6 us
    pallas_call x1, Pallas kernels, widen(): pl.pallas_call(widen_kernel, out_shape=(jax.ShapeDtypeStruct((CELLS, WIDT...  7.33 us

profile of v4, /device:TPU:1, one launch (start us, length us, event | category | flops | bytes accessed | tf_op | source)
XLA Modules:
  0.0 106.8 jit_solution(5933246142797508811)
XLA Ops:
  0.6 98.6 %shard_map.162 = (bf16[1024,1024]{1,0:T(8,128)(2,1)}, bf16[1024,1024]{1,0:T(8,128)(2,1)}, bf16[1024,1024]{1,0:T(8,128)(2,1)}, bf16[1024,256]{1,0:T(8,128)(2,1)}, f32[40,128]{1,0:T(8,128)}) custom-call(bf16[2048,128]{1,0:T(8,128)(2,1)} %values.1, s32[1,2048]{1,0:T(1,128)} %bitcast.8, s32[1,2048]{1,0:T(1,128)} %bitcast.9, s32[1,2048]{1,0:T(1,128)} %bitcast.10, ...), custom_call_target="tpu_custom_call" | custom-call | tf_op jit(solution)/shard_map/pallas_call | solution.py:756
  99.3 7.3 %shard_map.163 = (bf16[1024,1024]{1,0:T(8,128)(2,1)}, f32[1024,1024]{1,0:T(8,128)}, f32[1024,1024]{1,0:T(8,128)}, f32[128,1024]{1,0:T(8,128)}, f32[8,128]{1,0:T(...) custom-call(bf16[1024,1024]{1,0:T(8,128)(2,1)} %get-tuple-element.19.y, bf16[1024,1024]{1,0:T(8,128)(2,1)} %get-tuple-element.20.down, ...), custom_call_target="tpu_custom_call" | custom-call | tf_op jit(solution)/shard_map/pallas_call | solution.py:861

commit v5 on v4

--- a/solution.py
+++ b/solution.py
@@ -25,9 +25,9 @@
 
 
 PLAN = (
-    "gd0", 0, 1, "gd1", 0, 1, "gu0", 2, 3, 4, "gu1", 2, 3, 4, "b0", "b1", "b2", "b3", 0, 1, "i",
-    5, 2, 3, 4, 5, "f", 0, 1, "t", "s", 2, 3, 4, 5, "s", 0, 1, "y0", 2, 3, 4, 5, "s", "y1", 0,
-    1, 2, 3, 4, 5, "s", 0, 1, 2, 3, 4, 5, "s", 5,
+    "gd0", 0, 1, "gd1", 0, 1, "gu0", 2, 3, 4, "gu1", 2, 3, 4, "b0", "b1", "b2", "b3", "i", 5, 0,
+    1, 2, 3, 4, "f", 5, "t", "s", 0, 1, 2, 3, 4, "y0", 5, 0, 1, 2, 3, 4, "s", "y1", 5, 0, 1, 2,
+    3, 4, "s", 5, 0, 1, 2, 3, 4, "s", 5, 0, 1, 2, 3, 4, 5, "s", 5,
 )
 
 
@@ -69,27 +69,17 @@
         self.at, self.give, self.keep, self.o = at, give, keep, outs[output]
         half = self.o.shape[1] // 2
         self.out_cols = pl.ds(pl.multiple_of(at["core"] * half + first_out, 128), wide)
-        self.core_in, self.core_sum, self.axis_in, self.plane_in, self.axis_sum = bufs
+        self.core_in, self.core_sum, self.axis_in, self.axis_sum, self.next_in, self.last_in = bufs
         self.sends, self.recvs = send_sem.at[number], recv_sem.at[number]
-        self.mine = at[self.plane[0]] * 4 + at[self.plane[1]]
         self.done = 0
 
     def go(self, source, target, slot, at):
         send_to(source, target, self.sends.at[slot], self.recvs.at[slot], device_at(at))
 
-    def to_axis(self, slot, refs):
+    def to_axis(self, axis, slot, refs):
         for step in (1, 2, 3):
-            peer = moved(self.at, self.axis, step)
+            peer = moved(self.at, axis, step)
             self.go(*refs(step, peer), slot, peer)
-
-    def to_plane(self, slot, refs):
-        def body(step, carry):
-            peer = moved(self.at, self.plane[0], step // 4)
-            peer = moved(peer, self.plane[1], lax.rem(step, 4))
-            self.go(*refs(step, peer), slot, peer)
-            return carry
-
-        lax.fori_loop(1, 16, body, 0)
 
     def arrived(self, slot, ref):
         pltpu.make_async_copy(ref, ref, self.recvs.at[slot]).wait()
@@ -99,8 +89,8 @@
 
     def my_rows(self, size):
         start = self.at[self.axis] * 256
-        if size == 16:
-            start = start + self.mine * 16
+        if size == 64:
+            start = start + self.at[self.plane[0]] * 64
         return pl.ds(pl.multiple_of(start, size), size)
 
     def step0(self):
@@ -109,75 +99,68 @@
 
     def step1(self):
         self.arrived(0, self.core_in.at[:, self.cols])
-        size = 256
-
-        def body(i, carry):
-            rows = aligned(i, size)
+        for step in (1, 2, 3, 0):
+            peer = moved(self.at, self.axis, step)
+            rows = aligned(peer[self.axis], 256)
             total = self.keep[rows, self.cols].astype(f32) + self.core_in[rows, self.cols].astype(f32)
             self.core_sum[rows, self.cols] = total.astype(bf16)
-            return carry
-
-        lax.fori_loop(0, ROWS // size, body, 0)
-        self.to_axis(
-            1,
-            lambda step, peer: (
-                self.core_sum.at[aligned(peer[self.axis], 256), self.cols],
-                self.axis_in.at[step - 1, :, self.cols],
-            ),
-        )
+            if step:
+                landing = self.axis_in.at[step - 1, :, self.cols]
+                self.go(self.core_sum.at[rows, self.cols], landing, 1, peer)
 
     def step2(self):
         self.arrived(1, self.axis_in.at[:, :, self.cols])
-        size = 64
-
-        def body(i, carry):
-            rows = aligned(i, size)
-            own = pl.ds(pl.multiple_of(self.at[self.axis] * 256 + i * size, size), size)
+        for step in (1, 2, 3, 0):
+            peer = moved(self.at, self.plane[0], step)
+            part = peer[self.plane[0]]
+            rows = aligned(part, 64)
+            own = pl.ds(pl.multiple_of(self.at[self.axis] * 256 + part * 64, 64), 64)
             total = self.core_sum[own, self.cols].astype(f32)
             for j in range(3):
                 total = total + self.axis_in[j, rows, self.cols].astype(f32)
             self.axis_sum[rows, self.cols] = total.astype(bf16)
-            return carry
-
-        lax.fori_loop(0, 256 // size, body, 0)
-        self.to_plane(
-            2,
-            lambda step, peer: (
-                self.axis_sum.at[
-                    aligned(peer[self.plane[0]] * 4 + peer[self.plane[1]], 16), self.cols
-                ],
-                self.plane_in.at[step - 1, :, self.cols],
-            ),
-        )
+            if step:
+                landing = self.next_in.at[step - 1, :, self.cols]
+                self.go(self.axis_sum.at[rows, self.cols], landing, 2, peer)
 
     def step3(self):
-        self.arrived(2, self.plane_in.at[:, :, self.cols])
-        total = self.axis_sum[aligned(self.mine, 16), self.cols].astype(f32)
-        for j in range(15):
-            total = total + self.plane_in[j, :, self.cols].astype(f32)
-        self.o[self.my_rows(16), self.out_cols] = total.astype(bf16)
-        part = self.o.at[self.my_rows(16), self.out_cols]
-        self.to_plane(3, lambda step, peer: (part, part))
+        self.arrived(2, self.next_in.at[:, :, self.cols])
+        total = self.axis_sum[aligned(self.at[self.plane[0]], 64), self.cols].astype(f32)
+        for j in range(3):
+            total = total + self.next_in[j, :, self.cols].astype(f32)
+        mine = self.at[self.plane[1]]
+        self.last_in[mine, :, self.cols] = total.astype(bf16)
+        part = self.last_in.at[mine, :, self.cols]
+        self.to_axis(self.plane[1], 3, lambda step, peer: (part, part))
 
     def step4(self):
-        self.arrived(3, self.rows_of(240))
+        self.arrived(3, self.rows_of(192))
+        total = self.last_in[0, :, self.cols].astype(f32)
+        for j in range(1, 4):
+            total = total + self.last_in[j, :, self.cols].astype(f32)
+        self.o[self.my_rows(64), self.out_cols] = total.astype(bf16)
+        part = self.o.at[self.my_rows(64), self.out_cols]
+        self.to_axis(self.plane[0], 4, lambda step, peer: (part, part))
+
+    def step5(self):
+        self.arrived(4, self.rows_of(192))
         part = self.o.at[self.my_rows(256), self.out_cols]
-        self.to_axis(4, lambda step, peer: (part, part))
-
-    def step5(self):
-        self.arrived(4, self.rows_of(768))
+        self.to_axis(self.axis, 5, lambda step, peer: (part, part))
+
+    def step6(self):
+        self.arrived(5, self.rows_of(768))
         part = self.o.at[:, self.out_cols]
-        self.go(part, part, 5, moved(self.at, "core", 1))
-
-    def step6(self):
-        self.arrived(5, self.rows_of(ROWS))
+        self.go(part, part, 6, moved(self.at, "core", 1))
+
+    def step7(self):
+        self.arrived(6, self.rows_of(ROWS))
 
     def advance(self):
         getattr(self, "step" + str(self.done))()
         self.done += 1
 
     def finish(self):
-        for slot, rows in enumerate((ROWS, 768, 240, 240, 768, ROWS)):
+        for slot, rows in enumerate((ROWS, 768, 192, 192, 192, 768, ROWS)):
             ref = self.rows_of(rows)
             pltpu.make_async_copy(ref, ref, self.sends.at[slot]).wait()
 
@@ -187,10 +170,11 @@
         pltpu.VMEM((ROWS, HALF), bf16),
         pltpu.VMEM((ROWS, HALF), bf16),
         pltpu.VMEM((3, 256, HALF), bf16),
-        pltpu.VMEM((15, 16, HALF), bf16),
         pltpu.VMEM((256, HALF), bf16),
-        pltpu.SemaphoreType.DMA((len(STREAMS), 6)),
-        pltpu.SemaphoreType.DMA((len(STREAMS), 6)),
+        pltpu.VMEM((3, 64, HALF), bf16),
+        pltpu.VMEM((4, 64, HALF), bf16),
+        pltpu.SemaphoreType.DMA((len(STREAMS), 7)),
+        pltpu.SemaphoreType.DMA((len(STREAMS), 7)),
     ]
 
 
@@ -268,7 +252,6 @@
     places,
     packed,
     tags_out,
-    got,
     tags_in,
     lands,
     right,
@@ -307,9 +290,10 @@
     small_recv,
     core_in,
     core_sum,
-    in0,
-    in1,
-    out0,
+    axis_in,
+    axis_sum,
+    next_in,
+    last_in,
     send_sem,
     recv_sem,
 ):
@@ -399,11 +383,13 @@
 
     pl.semaphore_wait(rows_in, 15)
 
+    my_place = pl.ds(pl.multiple_of(lax.rem(me, SIDE) * CH + me // SIDE * SLOTS, SLOTS), SLOTS)
+
     def send_slot(source, landing, k, to_inst, to_tile):
         t = to_inst * 8 + to_tile
         pltpu.make_async_remote_copy(
             src_ref=source.at[t],
-            dst_ref=landing.at[me],
+            dst_ref=landing,
             send_sem=sems.at[k],
             recv_sem=sems.at[2 + k],
             device_id=(to_inst, to_tile),
@@ -412,7 +398,7 @@
 
     def send_tags(i, carry):
         peer = lax.rem(me + i * 37, DEVICES)
-        send_slot(tags_out, tags_in, 1, peer // 8, lax.rem(peer, 8))
+        send_slot(tags_out, tags_in.at[me], 1, peer // 8, lax.rem(peer, 8))
         return carry
 
     group = 8 * SLOTS
@@ -431,7 +417,7 @@
 
             @pl.when(to_inst * 8 + to_tile != me)
             def _():
-                send_slot(packed, got, 0, to_inst, to_tile)
+                send_slot(packed, right.at[my_place, :CH], 0, to_inst, to_tile)
 
             return inner_carry
 
@@ -442,7 +428,7 @@
         return carry
 
     lax.fori_loop(1, 17, pack_and_send, 0)
-    got[me] = packed[me]
+    right[my_place, :CH] = packed[me]
     tags_in[me] = tags_out[me]
     others = pl.ds(0, DEVICES - 1)
     pltpu.make_async_copy(tags_in.at[others], tags_in.at[others], sems.at[3]).wait()
@@ -482,15 +468,8 @@
     loads[0].wait()
     loads[1].wait()
     go_back(0)
-    pltpu.make_async_copy(got.at[others], got.at[others], sems.at[2]).wait()
-
-    def collect_rows(g, carry):
-        for m in range(4):
-            rows = pl.ds(pl.multiple_of(g * CH + m * SLOTS, SLOTS), SLOTS)
-            right[rows, :CH] = got[g + SIDE * m]
-        return carry
-
-    lax.fori_loop(0, SIDE, collect_rows, 0)
+    landed = right.at[pl.ds(0, (DEVICES - 1) * SLOTS), :CH]
+    pltpu.make_async_copy(landed, landed, sems.at[2]).wait()
 
     def sum_block(i, carry):
         total = jnp.dot(lands[aligned(i, half), :], right[...], preferred_element_type=f32)
@@ -569,7 +548,7 @@
 
     give, keep = lands.at[:, :HALF], lands.at[:, HALF : 2 * HALF]
     g = lands.at[:, 2 * HALF : 2 * HALF + WIDTH]
-    bufs = (core_in, core_sum, in0, in1, out0)
+    bufs = (core_in, core_sum, axis_in, axis_sum, next_in, last_in)
     outs = (o_down, o_up, o_in)
     streams = [
         Stream(k, at, give, keep, outs, bufs, send_sem, recv_sem) for k in range(len(STREAMS))
@@ -738,9 +717,9 @@
             tasks[task]()
             continue
         streams[task].advance()
-        if streams[0].done == 7 and streams[1].done == 7 and task in (0, 1):
+        if streams[0].done == 8 and streams[1].done == 8 and task in (0, 1):
             store(o_down, down_hbm)
-        if all(streams[k].done == 7 for k in (2, 3, 4)) and task in (2, 3, 4):
+        if all(streams[k].done == 8 for k in (2, 3, 4)) and task in (2, 3, 4):
             store(o_up, up_hbm)
     store(o_in, in_hbm)
     for s in streams:
@@ -769,7 +748,6 @@
             pltpu.VMEM((1, OBS_HERE), jnp.int32),
             pltpu.VMEM((DEVICES, SLOTS, CH), bf16),
             pltpu.VMEM((DEVICES, 1, CH), f32),
-            pltpu.VMEM((DEVICES, SLOTS, CH), bf16),
             pltpu.VMEM((DEVICES, 1, CH), f32),
             pltpu.VMEM((CELLS, DEVICES * SLOTS), bf16),
             pltpu.VMEM((DEVICES * SLOTS, 2 * CH), bf16),

time: 107 us -> 105 us (0.981)
  Pallas kernels: 106 us -> 104 us
    pallas_call x1, Pallas kernels: 98.6 us -> 96.6 us  [step(): pl.pallas_call(step_kernel, out_shape=(jax.ShapeDtypeStruct((CELLS, WIDTH...]
where the time goes in v5:
time: 105 us
  Pallas kernels  104 us (99%)
    pallas_call x1, Pallas kernels, step(): pl.pallas_call(step_kernel, out_shape=(jax.ShapeDtypeStruct((CELLS, WIDTH...  96.6 us
    pallas_call x1, Pallas kernels, widen(): pl.pallas_call(widen_kernel, out_shape=(jax.ShapeDtypeStruct((CELLS, WIDT...  7.33 us

profile of v5, /device:TPU:1, one launch (start us, length us, event | category | flops | bytes accessed | tf_op | source)
XLA Modules:
  0.0 104.8 jit_solution(1165111971049153782)
XLA Ops:
  0.6 96.6 %shard_map.162 = (bf16[1024,1024]{1,0:T(8,128)(2,1)}, bf16[1024,1024]{1,0:T(8,128)(2,1)}, bf16[1024,1024]{1,0:T(8,128)(2,1)}, bf16[1024,256]{1,0:T(8,128)(2,1)}, f32[40,128]{1,0:T(8,128)}) custom-call(bf16[2048,128]{1,0:T(8,128)(2,1)} %values.1, s32[1,2048]{1,0:T(1,128)} %bitcast.8, s32[1,2048]{1,0:T(1,128)} %bitcast.9, s32[1,2048]{1,0:T(1,128)} %bitcast.10, ...), custom_call_target="tpu_custom_call" | custom-call | tf_op jit(solution)/shard_map/pallas_call | solution.py:735
  97.3 7.3 %shard_map.163 = (bf16[1024,1024]{1,0:T(8,128)(2,1)}, f32[1024,1024]{1,0:T(8,128)}, f32[1024,1024]{1,0:T(8,128)}, f32[128,1024]{1,0:T(8,128)}, f32[8,128]{1,0:T(...) custom-call(bf16[1024,1024]{1,0:T(8,128)(2,1)} %get-tuple-element.19.y, bf16[1024,1024]{1,0:T(8,128)(2,1)} %get-tuple-element.20.down, ...), custom_call_target="tpu_custom_call" | custom-call | tf_op jit(solution)/shard_map/pallas_call | solution.py:839

commit v6 on v5

--- a/solution.py
+++ b/solution.py
@@ -25,7 +25,7 @@
 
 
 PLAN = (
-    "gd0", 0, 1, "gd1", 0, 1, "gu0", 2, 3, 4, "gu1", 2, 3, 4, "b0", "b1", "b2", "b3", "i", 5, 0,
+    "gd0", 0, 1, "gd1", 0, 1, "gu0", 2, 3, 4, "gu1", 2, 3, 4, "b0", "b1", "i", 5, 0,
     1, 2, 3, 4, "f", 5, "t", "s", 0, 1, 2, 3, 4, "y0", 5, 0, 1, 2, 3, 4, "s", "y1", 5, 0, 1, 2,
     3, 4, "s", 5, 0, 1, 2, 3, 4, "s", 5, 0, 1, 2, 3, 4, 5, "s", 5,
 )
@@ -556,11 +556,11 @@
     core = at["core"]
 
     def forward(i, carry):
-        rows = aligned(i, block)
+        rows = aligned(i, half)
         h = jnp.dot(enc[rows, :], w_in[...], preferred_element_type=f32)
         h0[rows, :] = h
         r = lax.rsqrt(jnp.mean(h * h, axis=-1, keepdims=True) + 1e-06)
-        rinv[rows, :] = jnp.broadcast_to(r, (block, CH))
+        rinv[rows, :] = jnp.broadcast_to(r, (half, CH))
         u_here = (h * r * gain[...]).astype(bf16)
         u[rows, :] = u_here
         for n in range(WIDTH // block):
@@ -576,7 +576,7 @@
             dact[rows, cols] = (slope * back[rows, cols]).astype(bf16)
         return carry
 
-    lax.fori_loop(0, CELLS // block, forward, 0)
+    lax.fori_loop(0, CELLS // half, forward, 0)
 
     def weight_grad(left, right_side, into, part, first):
         cols_in = aligned(part, 512)
@@ -593,7 +593,7 @@
     gain_sum[...] = jnp.zeros_like(gain_sum)
 
     def backward(i, carry):
-        rows = pl.ds(i * block, block)
+        rows = pl.ds(i * half, half)
         du = nt_dot(dact[rows, :], w_up[...])
         h = h0[rows, :]
         r = rinv[rows, :1]
@@ -603,8 +603,8 @@
         dh = (r * scaled - h * (r * r * r * mean) + dyb[rows, :].astype(f32)).astype(bf16)
         u[rows, :] = dh
         denc = nt_dot(dh, w_in[...])
-        eight = pl.ds(i * 8, 8)
-        ds[eight] = denc.reshape(8, SIDE, CH) * inv[eight]
+        lat = pl.ds(i * 16, 16)
+        ds[lat] = denc.reshape(16, SIDE, CH) * inv[lat]
         return carry
 
     def in_grad(i, carry):
@@ -703,8 +703,6 @@
         "gu1": lambda: weight_grad(u, dact, keep, core, 512),
         "b0": lambda: backward(0, 0),
         "b1": lambda: backward(1, 0),
-        "b2": lambda: backward(2, 0),
-        "b3": lambda: backward(3, 0),
         "i": lambda: lax.fori_loop(0, WIDTH // block, in_grad, 0),
         "f": take_filter,
         "t": take_small,

time: 105 us -> 104 us (level)
  no operation moved by 1% of the time
where the time goes in v6:
time: 104 us
  Pallas kernels  103 us (99%)
    pallas_call x1, Pallas kernels, step(): pl.pallas_call(step_kernel, out_shape=(jax.ShapeDtypeStruct((CELLS, WIDTH...  95.8 us
    pallas_call x1, Pallas kernels, widen(): pl.pallas_call(widen_kernel, out_shape=(jax.ShapeDtypeStruct((CELLS, WIDT...  7.33 us

profile of v6, /device:TPU:1, one launch (start us, length us, event | category | flops | bytes accessed | tf_op | source)
XLA Modules:
  0.0 103.9 jit_solution(13355559511666571273)
XLA Ops:
  0.6 95.8 %shard_map.162 = (bf16[1024,1024]{1,0:T(8,128)(2,1)}, bf16[1024,1024]{1,0:T(8,128)(2,1)}, bf16[1024,1024]{1,0:T(8,128)(2,1)}, bf16[1024,256]{1,0:T(8,128)(2,1)}, f32[40,128]{1,0:T(8,128)}) custom-call(bf16[2048,128]{1,0:T(8,128)(2,1)} %values.1, s32[1,2048]{1,0:T(1,128)} %bitcast.8, s32[1,2048]{1,0:T(1,128)} %bitcast.9, s32[1,2048]{1,0:T(1,128)} %bitcast.10, ...), custom_call_target="tpu_custom_call" | custom-call | tf_op jit(solution)/shard_map/pallas_call | solution.py:733
  96.4 7.3 %shard_map.163 = (bf16[1024,1024]{1,0:T(8,128)(2,1)}, f32[1024,1024]{1,0:T(8,128)}, f32[1024,1024]{1,0:T(8,128)}, f32[128,1024]{1,0:T(8,128)}, f32[8,128]{1,0:T(...) custom-call(bf16[1024,1024]{1,0:T(8,128)(2,1)} %get-tuple-element.19.y, bf16[1024,1024]{1,0:T(8,128)(2,1)} %get-tuple-element.20.down, ...), custom_call_target="tpu_custom_call" | custom-call | tf_op jit(solution)/shard_map/pallas_call | solution.py:837
